TPU v7x, 128 devices: a whole 4x4x4 slice. The times are simulated.
128 devices in a mesh: dp: 8 (over x, z_lo), seq: 16 (over y, z_hi, core).
Axes of the slice: x: 4, y: 4, z: 4 (z_hi: 2, z_lo: 2; z = z_hi * 2 + z_lo), core: 2. Of those that a mesh axis runs over, the one named last changes fastest.
Arguments:
- tokens: bfloat16 [8, 2048, 1024], P('dp', 'seq'), may hold values from -6 to 6
- norm_gains: bfloat16 [2, 1024], P(None, ('dp', 'seq')), may hold values from 0.5 to 1.5
- norm_biases: bfloat16 [2, 1024], P(None, ('dp', 'seq')), may hold values from -1.5 to 1.5
- w_qkv: bfloat16 [1024, 3072], P(('dp', 'seq')), may hold values from -0.1875 to 0.1875
- attn_biases: bfloat16 [2, 1024], P(None, ('dp', 'seq')), may hold values from -2.5 to 2.5
- w_out: bfloat16 [1024, 1024], P(('dp', 'seq')), may hold values from -3 to 3
- branch_biases: bfloat16 [2, 1024], P(None, ('dp', 'seq')), may hold values from -1.5 to 1.5
- w_fc: bfloat16 [1024, 4096], P(('dp', 'seq')), may hold values from -0.1875 to 0.1875
- fc_bias: bfloat16 [4096], P(('dp', 'seq')), may hold values from -2.5 to 2.5
- w_proj: bfloat16 [4096, 1024], P(('dp', 'seq')), may hold values from -0.09375 to 0.09375
- cotangent: bfloat16 [8, 2048, 1024], P('dp', 'seq'), may hold values from -6 to 6
Outputs:
- block_out: bfloat16 [8, 2048, 1024], P('dp', 'seq')
- input_grad: bfloat16 [8, 2048, 1024], P('dp', 'seq')
- grad_norm_gains: float32 [2, 1024], P(None, ('dp', 'seq'))
- grad_norm_biases: float32 [2, 1024], P(None, ('dp', 'seq'))
- grad_w_qkv: float32 [1024, 3072], P(('dp', 'seq'))
- grad_attn_biases: float32 [2, 1024], P(None, ('dp', 'seq'))
- grad_w_out: float32 [1024, 1024], P(('dp', 'seq'))
- grad_branch_biases: float32 [2, 1024], P(None, ('dp', 'seq'))
- grad_w_fc: float32 [1024, 4096], P(('dp', 'seq'))
- grad_fc_bias: float32 [4096], P(('dp', 'seq'))
- grad_w_proj: float32 [4096, 1024], P(('dp', 'seq'))
All inputs are finite; a program needn't handle non-finite values.
Results may differ from a plain program's by a relative error of at most 0.034.
Values may be sent and summed in bfloat16 or wider, within the bound.
A program may use at most 192 MiB of HBM per device.

v0:
```python
import math

import jax
import jax.numpy as jnp
from jax import lax
from jax.sharding import PartitionSpec as P

H = 16
HEAD = 64


epsilon = 1e-05
masked_score = -1e30


def layer_norm(inputs, scaling, offset):
    average = jnp.mean(inputs, axis=-1, keepdims=True)
    centred = inputs - average
    variance = jnp.mean(centred * centred, axis=-1, keepdims=True)
    return centred * lax.rsqrt(variance + epsilon) * scaling + offset


def gelu_tanh(inputs):
    return (
        0.5
        * inputs
        * (1.0 + jnp.tanh(0.7978845608028654 * (inputs + 0.044715 * inputs * inputs * inputs)))
    )


def sweep(state, key_piece, value_piece, query3, first_row):
    piece_rows = key_piece.shape[0]
    row_count = query3.shape[0]
    block_len = math.gcd(piece_rows, 512)
    keys3 = key_piece.reshape(piece_rows, H, HEAD)
    values3 = value_piece.reshape(piece_rows, H, HEAD)
    score_scale = 1.0 / math.sqrt(HEAD)
    query_pos = first_row + jnp.arange(row_count, dtype=jnp.int32)

    def sweep_advance(index, state_now):
        offset_in = index * block_len

        def sweep_update_block(current):
            running_max, running_sum, weighted = current
            key_block = lax.dynamic_slice_in_dim(keys3, offset_in, block_len, 0)
            value_block = lax.dynamic_slice_in_dim(values3, offset_in, block_len, 0)
            scores = (
                jnp.einsum("qhe,khe->hqk", query3, key_block, preferred_element_type=jnp.float32)
                * score_scale
            )
            allowed = (offset_in + jnp.arange(block_len, dtype=jnp.int32))[None, :] <= query_pos[
                :, None
            ]
            scores = jnp.where(allowed[None], scores, masked_score)
            new_max = jnp.maximum(running_max, jnp.max(scores, axis=-1))
            shrink = jnp.exp(running_max - new_max)
            probs = jnp.where(allowed[None], jnp.exp(scores - new_max[..., None]), 0.0)
            running_sum = running_sum * shrink + jnp.sum(probs, axis=-1)
            weighted = weighted * shrink[..., None] + jnp.einsum(
                "hqk,khe->hqe",
                probs.astype(jnp.bfloat16),
                value_block,
                preferred_element_type=jnp.float32,
            )
            return (new_max, running_sum, weighted)

        return lax.cond(
            offset_in <= first_row + row_count - 1,
            sweep_update_block,
            lambda unchanged: unchanged,
            state_now,
        )

    return lax.fori_loop(0, piece_rows // block_len, sweep_advance, state)


def back_sweep(query3, d_att3, logsum, row_dots, key_all, value_all, first_row):
    length = key_all.shape[0]
    model_width = key_all.shape[1]
    row_count = query3.shape[0]
    block_len = math.gcd(length, 512)
    keys3 = key_all.reshape(length, H, HEAD)
    values3 = value_all.reshape(length, H, HEAD)
    score_scale = 1.0 / math.sqrt(HEAD)
    query_pos = first_row + jnp.arange(row_count, dtype=jnp.int32)
    initial = (
        jnp.zeros((H, row_count, HEAD), jnp.float32),
        jnp.zeros((length, model_width), jnp.float32),
        jnp.zeros((length, model_width), jnp.float32),
    )

    def back_advance(index, state_now):
        block_start = index * block_len

        def back_update_block(current):
            d_query, key_grads, value_grads = current
            key_block = lax.dynamic_slice_in_dim(keys3, block_start, block_len, 0)
            value_block = lax.dynamic_slice_in_dim(values3, block_start, block_len, 0)
            scores = (
                jnp.einsum("qhe,khe->hqk", query3, key_block, preferred_element_type=jnp.float32)
                * score_scale
            )
            allowed = (block_start + jnp.arange(block_len, dtype=jnp.int32))[None, :] <= query_pos[
                :, None
            ]
            probs = jnp.where(allowed[None], jnp.exp(scores - logsum[..., None]), 0.0)
            d_probs = jnp.einsum(
                "qhe,khe->hqk", d_att3, value_block, preferred_element_type=jnp.float32
            )
            d_scores = (probs * (d_probs - row_dots[..., None])).astype(jnp.bfloat16)
            d_query = (
                d_query
                + jnp.einsum(
                    "hqk,khe->hqe", d_scores, key_block, preferred_element_type=jnp.float32
                )
                * score_scale
            )
            key_part = (
                jnp.einsum("hqk,qhe->khe", d_scores, query3, preferred_element_type=jnp.float32)
                * score_scale
            )
            value_part = jnp.einsum(
                "hqk,qhe->khe",
                probs.astype(jnp.bfloat16),
                d_att3,
                preferred_element_type=jnp.float32,
            )
            key_grads = lax.dynamic_update_slice_in_dim(
                key_grads, key_part.reshape(block_len, model_width), block_start, 0
            )
            value_grads = lax.dynamic_update_slice_in_dim(
                value_grads, value_part.reshape(block_len, model_width), block_start, 0
            )
            return (d_query, key_grads, value_grads)

        return lax.cond(
            block_start <= first_row + row_count - 1,
            back_update_block,
            lambda unchanged: unchanged,
            state_now,
        )

    return lax.fori_loop(0, length // block_len, back_advance, initial)


def on_device(
    tokens,
    norm_gains,
    norm_biases,
    w_qkv,
    attn_biases,
    w_out,
    branch_biases,
    w_fc,
    fc_bias,
    w_proj,
    cotangent,
):
    row_count = tokens.shape[1]
    model_width = tokens.shape[2]
    first_row = lax.axis_index("seq") * row_count
    inputs = tokens[0].astype(jnp.float32)
    qkv_all, out_all, gains_all, shifts_all, attn_bias_all, branch_bias_all = (
        lax.all_gather(w_qkv, ("dp", "seq"), axis=0, tiled=True),
        lax.all_gather(w_out, ("dp", "seq"), axis=0, tiled=True),
        lax.all_gather(norm_gains, ("dp", "seq"), axis=1, tiled=True),
        lax.all_gather(norm_biases, ("dp", "seq"), axis=1, tiled=True),
        lax.all_gather(attn_biases, ("dp", "seq"), axis=1, tiled=True),
        lax.all_gather(branch_biases, ("dp", "seq"), axis=1, tiled=True),
    )
    gains_f32 = gains_all.astype(jnp.float32)
    shifts_f32 = shifts_all.astype(jnp.float32)
    attn_bias_f32 = attn_bias_all.astype(jnp.float32)
    branch_bias_f32 = branch_bias_all.astype(jnp.float32)
    normed1, norm1_pull = jax.vjp(layer_norm, inputs, gains_f32[0], shifts_f32[0])
    hidden1 = normed1.astype(jnp.bfloat16)
    projected = jnp.dot(hidden1, qkv_all, preferred_element_type=jnp.float32)
    query = (projected[:, :model_width] + attn_bias_f32[0]).astype(jnp.bfloat16)
    keys = projected[:, model_width : 2 * model_width].astype(jnp.bfloat16)
    values = (projected[:, 2 * model_width :] + attn_bias_f32[1]).astype(jnp.bfloat16)
    query3 = query.reshape(row_count, H, HEAD)
    start_state = (
        jnp.full((H, row_count), masked_score, jnp.float32),
        jnp.zeros((H, row_count), jnp.float32),
        jnp.zeros((H, row_count, HEAD), jnp.float32),
    )
    state = sweep(
        start_state,
        lax.all_gather(keys, "seq", axis=0, tiled=True),
        lax.all_gather(values, "seq", axis=0, tiled=True),
        query3,
        first_row,
    )
    running_max, running_sum, weighted = state
    attn_f32 = weighted / running_sum[..., None]
    logsum = running_max + jnp.log(running_sum)
    attended = attn_f32.transpose(1, 0, 2).reshape(row_count, model_width).astype(jnp.bfloat16)
    branch = jnp.dot(attended, out_all, preferred_element_type=jnp.float32) + branch_bias_f32[0]
    middle = inputs + branch
    normed2, norm2_pull = jax.vjp(layer_norm, middle, gains_f32[1], shifts_f32[1])
    hidden2 = normed2.astype(jnp.bfloat16)
    fc_all, proj_all, fc_bias_all = (
        lax.all_gather(w_fc, ("dp", "seq"), axis=0, tiled=True),
        lax.all_gather(w_proj, ("dp", "seq"), axis=0, tiled=True),
        lax.all_gather(fc_bias, ("dp", "seq"), axis=0, tiled=True),
    )
    pre = jnp.dot(hidden2, fc_all, preferred_element_type=jnp.float32) + fc_bias_all.astype(
        jnp.float32
    )
    activated, gelu_pull = jax.vjp(gelu_tanh, pre)
    act = activated.astype(jnp.bfloat16)
    block_out = (
        middle + jnp.dot(act, proj_all, preferred_element_type=jnp.float32) + branch_bias_f32[1]
    )
    fc_back, proj_back = (
        lax.all_gather(w_fc, ("dp", "seq"), axis=0, tiled=True),
        lax.all_gather(w_proj, ("dp", "seq"), axis=0, tiled=True),
    )
    grad_out = cotangent[0]
    d_act = jnp.dot(grad_out, proj_back.T, preferred_element_type=jnp.float32)
    d_pre = gelu_pull(d_act)[0].astype(jnp.bfloat16)
    g_proj = jnp.dot(act.T, grad_out, preferred_element_type=jnp.float32)
    g_proj_bias = jnp.sum(grad_out.astype(jnp.float32), axis=0)
    g_fc = jnp.dot(hidden2.T, d_pre, preferred_element_type=jnp.float32)
    g_fc_bias = jnp.sum(d_pre.astype(jnp.float32), axis=0)
    d_hidden2 = jnp.dot(d_pre, fc_back.T, preferred_element_type=jnp.float32)
    d_middle_norm, g_gain2, g_shift2 = norm2_pull(d_hidden2)
    d_middle = grad_out.astype(jnp.float32) + d_middle_norm
    fc_grad, proj_grad, fc_bias_grad = (
        lax.psum_scatter(g_fc, ("dp", "seq"), scatter_dimension=0, tiled=True),
        lax.psum_scatter(g_proj, ("dp", "seq"), scatter_dimension=0, tiled=True),
        lax.psum_scatter(g_fc_bias, ("dp", "seq"), scatter_dimension=0, tiled=True),
    )
    qkv_back, out_back = (
        lax.all_gather(w_qkv, ("dp", "seq"), axis=0, tiled=True),
        lax.all_gather(w_out, ("dp", "seq"), axis=0, tiled=True),
    )
    d_branch = d_middle.astype(jnp.bfloat16)
    g_out = jnp.dot(attended.T, d_branch, preferred_element_type=jnp.float32)
    g_out_bias = jnp.sum(d_branch.astype(jnp.float32), axis=0)
    d_attended = jnp.dot(d_branch, out_back.T, preferred_element_type=jnp.float32).astype(
        jnp.bfloat16
    )
    d_att3 = d_attended.reshape(row_count, H, HEAD)
    row_dots = jnp.sum(d_att3.astype(jnp.float32).transpose(1, 0, 2) * attn_f32, axis=-1)
    key_back, value_back = (
        lax.all_gather(keys, "seq", axis=0, tiled=True),
        lax.all_gather(values, "seq", axis=0, tiled=True),
    )
    d_query, key_grads, value_grads = back_sweep(
        query3, d_att3, logsum, row_dots, key_back, value_back, first_row
    )
    key_mine, value_mine = (
        lax.psum_scatter(
            key_grads.astype(jnp.bfloat16), "seq", scatter_dimension=0, tiled=True
        ).astype(jnp.float32),
        lax.psum_scatter(
            value_grads.astype(jnp.bfloat16), "seq", scatter_dimension=0, tiled=True
        ).astype(jnp.float32),
    )
    d_query_low = d_query.transpose(1, 0, 2).reshape(row_count, model_width).astype(jnp.bfloat16)
    d_value_low = value_mine.astype(jnp.bfloat16)
    d_qkv = jnp.concatenate([d_query_low, key_mine.astype(jnp.bfloat16), d_value_low], axis=1)
    g_qkv = jnp.dot(hidden1.T, d_qkv, preferred_element_type=jnp.float32)
    g_attn_bias = jnp.stack(
        [
            jnp.sum(d_query_low.astype(jnp.float32), axis=0),
            jnp.sum(d_value_low.astype(jnp.float32), axis=0),
        ]
    )
    d_hidden1 = jnp.dot(d_qkv, qkv_back.T, preferred_element_type=jnp.float32)
    d_input_norm, g_gain1, g_shift1 = norm1_pull(d_hidden1)
    input_grad = (d_middle + d_input_norm).astype(jnp.bfloat16)
    g_gains = jnp.stack([g_gain1, g_gain2])
    g_shifts = jnp.stack([g_shift1, g_shift2])
    g_branch_bias = jnp.stack([g_out_bias, g_proj_bias])
    qkv_grad, out_grad, gains_grad, shifts_grad, attn_bias_grad, branch_bias_grad = (
        lax.psum_scatter(g_qkv, ("dp", "seq"), scatter_dimension=0, tiled=True),
        lax.psum_scatter(g_out, ("dp", "seq"), scatter_dimension=0, tiled=True),
        lax.psum_scatter(g_gains, ("dp", "seq"), scatter_dimension=1, tiled=True),
        lax.psum_scatter(g_shifts, ("dp", "seq"), scatter_dimension=1, tiled=True),
        lax.psum_scatter(g_attn_bias, ("dp", "seq"), scatter_dimension=1, tiled=True),
        lax.psum_scatter(g_branch_bias, ("dp", "seq"), scatter_dimension=1, tiled=True),
    )
    return (
        block_out.astype(jnp.bfloat16)[None],
        input_grad[None],
        gains_grad,
        shifts_grad,
        qkv_grad,
        attn_bias_grad,
        out_grad,
        branch_bias_grad,
        fc_grad,
        fc_bias_grad,
        proj_grad,
    )


def solution(mesh):
    in_specs = (
        P("dp", "seq", None),
        P(None, ("dp", "seq")),
        P(None, ("dp", "seq")),
        P(("dp", "seq"), None),
        P(None, ("dp", "seq")),
        P(("dp", "seq"), None),
        P(None, ("dp", "seq")),
        P(("dp", "seq"), None),
        P(("dp", "seq")),
        P(("dp", "seq"), None),
        P("dp", "seq", None),
    )
    out_specs = (
        P("dp", "seq", None),
        P("dp", "seq", None),
        P(None, ("dp", "seq")),
        P(None, ("dp", "seq")),
        P(("dp", "seq"), None),
        P(None, ("dp", "seq")),
        P(("dp", "seq"), None),
        P(None, ("dp", "seq")),
        P(("dp", "seq"), None),
        P(("dp", "seq")),
        P(("dp", "seq"), None),
    )
    return jax.shard_map(
        on_device, mesh=mesh, in_specs=in_specs, out_specs=out_specs, check_vma=False
    )
```

profile of v0, /device:TPU:1, one launch (start us, length us, event | category | flops | bytes accessed | tf_op | source)
XLA Modules:
  0.0 4116.8 jit_solution(3730164753295474354)
XLA Ops:
  8.0 179.5 %all-gather = bf16[128,8,2]{1,2,0:T(2,128)(2,1)S(1)} all-gather(bf16[1,8,2]{1,2,0:T(2,128)(2,1)} %bitcast.206), channel_id=1, replica_groups=mesh['dp'=8,'seq'=16] {'dp','seq'}, dimensions={0}, use_global_device_ids=true | all-gather | bytes 4128 | tf_op jit(solution)/shard_map/all_gather | solution.py:166
  187.5 169.8 %all-gather.1 = bf16[128,8,2]{1,2,0:T(2,128)(2,1)S(1)} all-gather(bf16[1,8,2]{1,2,0:T(2,128)(2,1)} %bitcast.207), channel_id=1, replica_groups=mesh['dp'=8,'seq'=16] {'dp','seq'}, dimensions={0}, use_global_device_ids=true | all-gather | bytes 4128 | tf_op jit(solution)/shard_map/all_gather | solution.py:167
  357.4 172.7 %all-gather.2 = bf16[128,8,2]{1,2,0:T(2,128)(2,1)S(1)} all-gather(bf16[1,8,2]{1,2,0:T(2,128)(2,1)} %bitcast.208), channel_id=1, replica_groups=mesh['dp'=8,'seq'=16] {'dp','seq'}, dimensions={0}, use_global_device_ids=true | all-gather | bytes 4128 | tf_op jit(solution)/shard_map/all_gather | solution.py:168
  533.3 4.0 fusion.80
  541.0 67.8 %all-reduce = bf16[4096]{0:T(1024)(128)(2,1)S(1)} all-reduce(bf16[4096]{0:T(1024)(128)(2,1)S(1)} %dynamic-update-slice), channel_id=1, replica_groups=mesh['dp'=8,'seq'=16] {'dp','seq'}, use_global_device_ids=true, to_apply=%add | all-reduce | flops 4096 | bytes 16384
  608.8 173.8 %all-gather.3 = bf16[128,8,2]{1,2,0:T(2,128)(2,1)S(1)} all-gather(bf16[1,8,2]{1,2,0:T(2,128)(2,1)S(1)} %bitcast.209), channel_id=1, replica_groups=mesh['dp'=8,'seq'=16] {'dp','seq'}, dimensions={0}, use_global_device_ids=true | all-gather | bytes 4128 | tf_op jit(solution)/shard_map/all_gather | solution.py:169
  783.1 6.5 copy.70
  789.6 6.5 copy.66
  796.2 6.6 while.40
  796.2 6.2 conditional.6
  802.8 37.1 all-gather.17.cloned.1.call-done
  842.3 200.8 %all-gather.19.cloned.1.call-done = bf16[1024,4096]{1,0:T(8,128)(2,1)} async-done(((bf16[8,4096]{1,0:T(8,128)(2,1)}), bf16[1024,4096]{1,0:T(8,128)(2,1)}) %all-gather.19.cloned.1.call-update) | async-done | bytes 8388624 | tf_op jit(solution)/shard_map/all_gather | solution.py:203
  1043.1 6.1 convolution_add_fusion
  1049.2 197.2 %all-gather.21.cloned.1.call-done = bf16[4096,1024]{1,0:T(8,128)(2,1)} async-done(((bf16[32,1024]{1,0:T(8,128)(2,1)}), bf16[4096,1024]{1,0:T(8,128)(2,1)}) %all-gather.21.cloned.1.call-update) | async-done | bytes 8388624 | tf_op jit(solution)/shard_map/all_gather | solution.py:204
  1246.3 8.3 convert_reduce_fusion
  1254.6 3.0 multiply_reduce_fusion
  1265.0 10.6 while.41
  1265.2 10.3 conditional.7
  1275.6 6.4 copy.80
  1282.0 6.4 copy.78
  1291.6 98.6 %reduce-scatter.25.cloned.1.call-done = bf16[128,1024]{1,0:T(8,128)(2,1)} async-done(((bf16[2048,1024]{1,0:T(8,128)(2,1)}), bf16[128,1024]{1,0:T(8,128)(2,1)}) %reduce-scatter.25.cloned.1.call-update) | async-done | bytes 262160
  1391.3 82.5 %reduce-scatter.23.cloned.1.call-done = bf16[128,1024]{1,0:T(8,128)(2,1)} async-done(((bf16[2048,1024]{1,0:T(8,128)(2,1)}), bf16[128,1024]{1,0:T(8,128)(2,1)}) %reduce-scatter.23.cloned.1.call-update) | async-done | bytes 262160
  1474.9 6.4 fusion.65
  1481.4 9.7 fusion.68
  1492.4 8.2 fusion.83
  1500.6 6.3 fusion.48
  1507.2 5.1 fusion.84
  1513.7 67.0 %all-reduce.6 = (f32[2,1024]{1,0:T(2,128)S(1)}, f32[2,1024]{1,0:T(2,128)S(1)}, f32[2,1024]{1,0:T(2,128)S(1)}, f32[2,1024]{1,0:T(2,128)S(1)}, f32[4096]{0:T(1024)S(1)}) all-reduce(f32[2,1024]{1,0:T(2,128)S(1)} %pad_maximum_fusion.3, f32[2,1024]{1,0:T(2,128)S(1)} %pad_maximum_fusion.4, ...), channel_id=4, replica_groups=mesh['dp'=8,'seq'=16] {'dp','seq'}, use_global_device_ids=true, to_apply=%region_23.24.clone | all-reduce | flops 12288 | bytes 98304
  1582.6 530.0 %reduce-scatter.17.cloned.1.call-done = f32[8,1024]{1,0:T(8,128)} async-done(((f32[1024,1024]{1,0:T(8,128)}), f32[8,1024]{1,0:T(8,128)}) %reduce-scatter.17.cloned.1.call-update) | async-done | bytes 32784 | tf_op jit(solution)/shard_map/reduce_scatter | solution.py:279
  2112.6 657.4 %reduce-scatter.15.cloned.1.call-done = f32[8,3072]{1,0:T(8,128)} async-done(((f32[1024,3072]{1,0:T(8,128)}), f32[8,3072]{1,0:T(8,128)}) %reduce-scatter.15.cloned.1.call-update) | async-done | bytes 98320 | tf_op jit(solution)/shard_map/reduce_scatter | solution.py:278
  2770.0 669.0 %reduce-scatter.21.cloned.1.call-done = f32[32,1024]{1,0:T(8,128)} async-done(((f32[4096,1024]{1,0:T(8,128)}), f32[32,1024]{1,0:T(8,128)}) %reduce-scatter.21.cloned.1.call-update) | async-done | bytes 131088 | tf_op jit(solution)/shard_map/reduce_scatter | solution.py:231
  3439.1 670.6 %reduce-scatter.19.cloned.1.call-done = f32[8,4096]{1,0:T(8,128)} async-done(((f32[1024,4096]{1,0:T(8,128)}), f32[8,4096]{1,0:T(8,128)}) %reduce-scatter.19.cloned.1.call-update) | async-done | bytes 131088 | tf_op jit(solution)/shard_map/reduce_scatter | solution.py:230
  (149 shorter events, 44.4 us)
Async XLA Ops:
  7.2 526.1 %all-gather.11.cloned.1.call-start = ((), (), s32[]{:S(2)}) async-start(), calls=%async_computation.6 | async-start | bytes 6340608 | tf_op jit(solution)/shard_map/all_gather | solution.py:164
  7.9 775.2 %all-gather.15.cloned.1.call-start = ((), (), s32[]{:S(2)}) async-start(), calls=%async_computation.8 | async-start | bytes 4456448 | tf_op jit(solution)/shard_map/all_gather | solution.py:190
  533.3 7.5 copy-start.13
  533.3 75.5 %copy-start.12 = (bf16[2,8]{1,0:T(2,128)(2,1)S(1)}, bf16[2,8]{1,0:T(2,128)(2,1)}, u32[]{:S(2)}) copy-start(bf16[2,8]{1,0:T(2,128)(2,1)} %param.25) | copy-start | bytes 100
  538.1 251.5 %all-gather.13.cloned.1.call-start = ((), (), s32[]{:S(2)}) async-start(), calls=%async_computation.7 | async-start | bytes 4456448 | tf_op jit(solution)/shard_map/all_gather | solution.py:189
  538.9 301.0 %all-gather.17.cloned.1.call-start = ((), (), s32[]{:S(2)}) async-start(), calls=%async_computation.9 | async-start | bytes 2113536 | tf_op jit(solution)/shard_map/all_gather | solution.py:165
  539.5 503.6 %all-gather.19.cloned.1.call-start = ((), (), s32[]{:S(2)}) async-start(), calls=%async_computation.10 | async-start | bytes 8454144 | tf_op jit(solution)/shard_map/all_gather | solution.py:203
  540.1 706.2 %all-gather.21.cloned.1.call-start = ((), (), s32[]{:S(2)}) async-start(), calls=%async_computation.11 | async-start | bytes 8454144 | tf_op jit(solution)/shard_map/all_gather | solution.py:204
  540.7 849.5 %reduce-scatter.25.cloned.1.call-start = ((), (), s32[]{:S(2)}) async-start(), calls=%async_computation.17 | async-start | bytes 4456448
  796.2 43.7 %copy-start.1 = (bf16[1,128,1024]{2,1,0:T(8,128)(2,1)S(1)}, bf16[1,128,1024]{2,1,0:T(8,128)(2,1)}, u32[]{:S(2)}) copy-start(bf16[1,128,1024]{2,1,0:T(8,128)(2,1)} %param.19) | copy-start | bytes 786436
  1043.1 203.2 %copy-start.5 = (bf16[1,128,1024]{2,1,0:T(8,128)(2,1)S(1)}, bf16[1,128,1024]{2,1,0:T(8,128)(2,1)}, u32[]{:S(2)}) copy-start(bf16[1,128,1024]{2,1,0:T(8,128)(2,1)} %param.29) | copy-start | bytes 786436
  1246.3 8.3 copy-start
  1254.6 3.1 copy-start.3
  1254.6 3.5 copy-start.2
  1259.1 0.7 copy-start.8
  1260.0 5.0 copy-start.9
  1282.0 191.8 %reduce-scatter.23.cloned.1.call-start = ((), (), s32[]{:S(2)}) async-start(), calls=%async_computation.16 | async-start | bytes 4456448
  1288.5 824.1 %reduce-scatter.17.cloned.1.call-start = ((), (), s32[]{:S(2)}) async-start(), calls=%async_computation.13 | async-start | bytes 4227072 | tf_op jit(solution)/shard_map/reduce_scatter | solution.py:279
  1291.3 1478.7 %reduce-scatter.15.cloned.1.call-start = ((), (), s32[]{:S(2)}) async-start(), calls=%async_computation.12 | async-start | bytes 12681216 | tf_op jit(solution)/shard_map/reduce_scatter | solution.py:278
  1291.6 189.7 %copy-start.6 = (bf16[16,128,64]{1,2,0:T(8,128)(2,1)}, bf16[16,128,64]{1,2,0:T(8,128)(2,1)S(1)}, u32[]{:S(2)}) copy-start(bf16[16,128,64]{1,2,0:T(8,128)(2,1)S(1)} %get-tuple-element.751) | copy-start | bytes 786436
  1474.9 6.5 copy-start.10
  1481.4 1957.7 %reduce-scatter.21.cloned.1.call-start = ((), (), s32[]{:S(2)}) async-start(), calls=%async_computation.15 | async-start | bytes 16908288 | tf_op jit(solution)/shard_map/reduce_scatter | solution.py:231
  1491.1 1.2 copy-start.4
  1491.2 2618.5 %reduce-scatter.19.cloned.1.call-start = ((), (), s32[]{:S(2)}) async-start(), calls=%async_computation.14 | async-start | bytes 16908288 | tf_op jit(solution)/shard_map/reduce_scatter | solution.py:230
  1500.6 6.5 copy-start.7
  1500.6 6.5 copy-start.11
Sparse Core Ops, SparseCore 0:
  9.7 204.0 all-gather.10
  538.2 50.0 all-gather.14
  591.3 54.7 all-gather.12
  647.6 192.2 all-gather.16
  841.5 201.5 all-gather.18
  1044.7 201.5 all-gather.20
  1282.1 108.0 reduce-scatter.24
  1394.8 78.9 reduce-scatter.22
  1476.7 635.8 reduce-scatter.16
  2115.5 654.4 reduce-scatter.14
  2773.0 666.0 reduce-scatter.20
  3441.9 667.7 reduce-scatter.18
where the time goes:
time: 4130 us; the launch traced here: 4120 us
  waiting for transfers between devices  3150 us (76%)
  blocking collectives  831 us (20%)
  matrix products  76.3 us (2%)
    reduce_scatter x1, waiting for transfers between devices, on_device(): lax.psum_scatter(g_fc, ('dp', 'seq'), scatter_dimension=0, tiled=True)  671 us
    reduce_scatter x1, waiting for transfers between devices, on_device(): lax.psum_scatter(g_proj, ('dp', 'seq'), scatter_dimension=0, tiled=True)  669 us
    reduce_scatter x1, waiting for transfers between devices, on_device(): lax.psum_scatter(g_qkv, ('dp', 'seq'), scatter_dimension=0, tiled=True)  657 us
    reduce_scatter x1, waiting for transfers between devices, on_device(): lax.psum_scatter(g_out, ('dp', 'seq'), scatter_dimension=0, tiled=True)  530 us
    all_gather x1, waiting for transfers between devices, on_device(): lax.all_gather(w_fc, ('dp', 'seq'), axis=0, tiled=True)  201 us
    all_gather x1, waiting for transfers between devices, on_device(): lax.all_gather(w_proj, ('dp', 'seq'), axis=0, tiled=True)  197 us
    unnamed x14, waiting for transfers between devices  183 us
    all_gather x1, blocking collectives, on_device(): lax.all_gather(norm_gains, ('dp', 'seq'), axis=1, tiled=True)  180 us
  transfers between devices with their start and end apart: 12, of which 9 were waited for; matrix products, arithmetic and copies ran while one was open for 2% of the time, Pallas kernels for 0%

commit v1 on v0

v1 whole, which is shorter than its diff:
```python
import functools
import math

import jax
import jax.numpy as jnp
from jax import lax
from jax.experimental import pallas as pl
from jax.experimental.pallas import tpu as pltpu
from jax.sharding import PartitionSpec as P

MESH = pl.DeviceIdType.MESH
BF16 = jnp.bfloat16
F32 = jnp.float32

H = 16
HEAD = 64
D = 1024
FF = 4096
T = 256
LEN = 2048
HALF = D // 2
FFH = FF // 2
EPS = 1e-05
LOW = -1e30
SCALE2 = math.log2(math.e) / math.sqrt(HEAD)

SMALL0 = 3 * HALF
OUT0 = SMALL0 + 128
FC0 = OUT0 + HALF
W4 = FC0 + FFH
GOUT0 = 3 * HALF
GFC0 = GOUT0 + HALF
G4 = GFC0 + FFH

JB = 512
IB = 256

ORDERS = (("x", "y", "z"), ("y", "z", "x"), ("z", "x", "y"))
SIZES = {"x": 4, "y": 4, "z": 4}


def nt(a, b):
    return lax.dot_general(a, b, (((1,), (1,)), ((), ())), preferred_element_type=F32)


def nn(a, b):
    return jnp.dot(a, b, preferred_element_type=F32)


def mod4(v):
    return lax.rem(v + 4, 4)


def dev(co, core):
    x, y, z = co["x"], co["y"], co["z"]
    return (x * 2 + lax.rem(z, 2), y * 4 + lax.div(z, 2) * 2 + core)


def shift(co, axis, d):
    out = dict(co)
    out[axis] = mod4(co[axis] + d)
    return out


def blocks(ref, sel, c0, n):
    s = slice(None)
    x, y, z = sel["x"], sel["y"], sel["z"]
    return ref.at[
        s if x is None else x,
        s if z is None else lax.rem(z, 2),
        s if y is None else y,
        s if z is None else lax.div(z, 2),
        :,
        pl.ds(c0, n),
    ]


def lead_dims(fixed):
    out = []
    if "x" not in fixed:
        out.append(4)
    if "z" not in fixed:
        out.append(2)
    if "y" not in fixed:
        out.append(4)
    if "z" not in fixed:
        out.append(2)
    return tuple(out)


def half_split(n):
    first = ((n // 128) + 1) // 2 * 128
    return ((0, first), (first, n - first))


def way(d):
    return 0 if d > 0 else 1


class Piece:
    def __init__(self, me, core, ref, c0, n, rot, ssem, rsem, base):
        self.me, self.core, self.ref, self.c0, self.n = me, core, ref, c0, n
        self.order = ORDERS[rot]
        self.ssem, self.rsem, self.base = ssem, rsem, base

    def cols(self, h):
        if h is None:
            return self.c0, self.n
        off, n = half_split(self.n)[h]
        return self.c0 + off, n

    def remote(self, src, dst, ph, st, d):
        i = self.base + ph * 4 + st * 2 + way(d)
        return pltpu.make_async_remote_copy(
            src_ref=src,
            dst_ref=dst,
            send_sem=self.ssem.at[i],
            recv_sem=self.rsem.at[i],
            device_id=dev(shift(self.me, self.order[ph], d), self.core),
            device_id_type=MESH,
        )

    def ways(self, st):
        return (1, -1)


class Gather(Piece):
    def region(self, ph, off, h):
        sel = {}
        for k, a in enumerate(self.order):
            sel[a] = None if k < ph else (mod4(self.me[a] + off) if k == ph else self.me[a])
        return blocks(self.ref, sel, *self.cols(h))

    def copy(self, ph, st, d):
        r = self.region(ph, 0, None) if st == 0 else self.region(ph, -d, way(d))
        return self.remote(r, r, ph, st, d)

    def start(self, ph):
        for d in (1, -1):
            self.copy(ph, 0, d).start()

    def forward(self, ph):
        for d in (1, -1):
            r = self.region(ph, -d, None)
            self.remote(r, r, ph, 0, d).wait_recv()
            self.copy(ph, 1, d).start()

    def finish(self, ph):
        for d in (1, -1):
            r = self.region(ph, -2 * d, way(d))
            self.remote(r, r, ph, 1, d).wait_recv()

    def drain(self):
        for ph in range(3):
            for st in range(2):
                for d in (1, -1):
                    self.copy(ph, st, d).wait_send()


class Reduce(Piece):
    def attach(self, stage):
        self.stage = stage
        return self

    @staticmethod
    def stage_shapes(rows, n, rot, dtype):
        out = []
        (_, n0), (_, n1) = half_split(n)
        for ph in range(3):
            lead = lead_dims(ORDERS[rot][: ph + 1])
            out.append(pltpu.VMEM(lead + (rows, n0), dtype))
            out.append(pltpu.VMEM(lead + (rows, max(n1, 128)), dtype))
            out.append(pltpu.VMEM((2,) + lead + (rows, n), dtype))
        return out

    def region(self, ph, off, h):
        sel = {}
        for k, a in enumerate(self.order):
            sel[a] = self.me[a] if k < ph else (mod4(self.me[a] + off) if k == ph else None)
        return blocks(self.ref, sel, *self.cols(h))

    def ways0(self):
        return (1, -1) if self.n > 128 else (1,)

    def copy(self, ph, st, d):
        if st == 0:
            return self.remote(self.region(ph, 2, way(d)), self.stage[3 * ph + way(d)], ph, 0, d)
        return self.remote(self.region(ph, d, None), self.stage[3 * ph + 2].at[way(d)], ph, 1, d)

    def start(self, ph):
        for d in self.ways0():
            self.copy(ph, 0, d).start()

    def add(self, target, sources, lead):
        def one(idx):
            total = target[idx].astype(F32)
            for s in sources:
                total = total + s[idx].astype(F32)
            target[idx] = total.astype(target.dtype)

        if not lead:
            one(Ellipsis)
        else:
            lax.fori_loop(0, lead[0], lambda i, c: (one(i), c)[1], 0)

    def forward(self, ph):
        lead = lead_dims(self.order[: ph + 1])
        for d in (1, -1):
            if d in self.ways0():
                self.copy(ph, 0, d).wait_recv()
                self.add(self.region(ph, d, way(d)), [self.stage[3 * ph + way(d)]], lead)
            self.copy(ph, 1, d).start()

    def finish(self, ph, out=None):
        lead = lead_dims(self.order[: ph + 1])
        s = self.stage[3 * ph + 2]
        for d in (1, -1):
            self.copy(ph, 1, d).wait_recv()
        mine = self.region(ph, 0, None)
        if out is None:
            self.add(mine, [s.at[0], s.at[1]], lead)
        else:
            out[...] = mine[...].astype(F32) + s[0].astype(F32) + s[1].astype(F32)

    def drain(self):
        for ph in range(3):
            for d in self.ways0():
                self.copy(ph, 0, d).wait_send()
            for d in (1, -1):
                self.copy(ph, 1, d).wait_send()


GATHER_A = (("w4", 0, HALF, 0), ("w4", HALF, HALF, 1), ("w4", 2 * HALF, HALF + 128, 2))
GATHER_B = (
    ("w4", OUT0, HALF + 1024, 0),
    ("w4", FC0 + 1024, 1024, 1),
    ("wp", 768, 256, 1),
    ("wp", 0, 768, 2),
)
REDUCE_F = (
    ("g4", GFC0, 1280, 0),
    ("g4", GFC0 + 1280, 768, 1),
    ("gp", 0, 256, 1),
    ("gp", 256, 768, 2),
)
REDUCE_Q = (("g4", 0, 640, 0), ("g4", 640, 640, 1), ("g4", 1280, 768, 2), ("gs", 0, 128, 0))
ROWS = {"g4": 16, "gp": 32, "gs": 8}
TYPES = {"g4": BF16, "gp": BF16, "gs": F32}


def rows_loop(total, step, body, init=0):
    def one(i, c):
        return body(pl.ds(pl.multiple_of(i * step, step), step), c)

    return lax.fori_loop(0, total // step, one, init)


def fold8(v):
    return jnp.sum(v.reshape(v.shape[0] // 8, 8, v.shape[1]), axis=0)


def norm_stats(v):
    average = jnp.mean(v, axis=-1, keepdims=True)
    centred = v - average
    variance = jnp.mean(centred * centred, axis=-1, keepdims=True)
    inv = lax.rsqrt(variance + EPS)
    return centred * inv, inv


def norm_back(xhat, inv, dh, gain):
    a = dh * gain
    return inv * (
        a - jnp.mean(a, axis=-1, keepdims=True) - xhat * jnp.mean(a * xhat, axis=-1, keepdims=True)
    )


SCRATCH = dict(
    w4=pltpu.VMEM((4, 2, 4, 2, 16, W4), BF16),
    wp=pltpu.VMEM((4, 2, 4, 2, 32, D), BF16),
    g4=pltpu.VMEM((4, 2, 4, 2, 16, G4), BF16),
    gp=pltpu.VMEM((4, 2, 4, 2, 32, D), BF16),
    gs=pltpu.VMEM((4, 2, 4, 2, 8, 128), F32),
    wrecv=pltpu.VMEM((8, W4), F32),
    wor=pltpu.VMEM((2, 2, 4, 2, 16, D), BF16),
    x=pltpu.VMEM((T, D), BF16),
    dy=pltpu.VMEM((T, D), BF16),
    h1=pltpu.VMEM((T, D), BF16),
    h2=pltpu.VMEM((T, D), BF16),
    h2t=pltpu.VMEM((D, T), BF16),
    vec=pltpu.VMEM((8, D), F32),
    fcb=pltpu.VMEM((8, FFH), F32),
    qkvs=pltpu.VMEM((3, 8, HEAD, T), BF16),
    qkvt=pltpu.VMEM((3, HEAD, LEN), BF16),
    qz=pltpu.VMEM((2 * HEAD, LEN), BF16),
    dz=pltpu.VMEM((2 * HEAD, LEN), BF16),
    kv=pltpu.VMEM((LEN, 2 * HEAD), BF16),
    qd=pltpu.VMEM((LEN, 2 * HEAD), BF16),
    sbuf=pltpu.VMEM((LEN, IB), F32),
    ot=pltpu.VMEM((HEAD, LEN), F32),
    ots=pltpu.VMEM((HEAD, LEN), BF16),
    lse=pltpu.VMEM((8, LEN), F32),
    rowdot=pltpu.VMEM((8, LEN), F32),
    attt=pltpu.VMEM((8, HEAD, T), BF16),
    part=pltpu.VMEM((T, D), F32),
    partr=pltpu.VMEM((T, D), F32),
    middle=pltpu.VMEM((T, D), F32),
    outp=pltpu.VMEM((T, D), F32),
    outr=pltpu.VMEM((T // 2, D), F32),
    dh=pltpu.VMEM((T, D), F32),
    dhr=pltpu.VMEM((T, D), F32),
    dbr=pltpu.VMEM((T, D), BF16),
    datt=pltpu.VMEM((8, HEAD, T), BF16),
    dqkvt=pltpu.VMEM((3, HEAD, LEN), BF16),
    dqs=pltpu.VMEM((3, 8, HEAD, T), BF16),
    dh1r=pltpu.VMEM((T // 2, D), F32),
    sv=pltpu.VMEM((8, D), F32),
    sfc=pltpu.VMEM((8, FFH), F32),
    fin=pltpu.VMEM((16, G4), F32),
    fins=pltpu.VMEM((8, 128), F32),
    finr=pltpu.VMEM((8, 128), F32),
    ag_s=pltpu.SemaphoreType.DMA((12 * 7,)),
    ag_r=pltpu.SemaphoreType.DMA((12 * 7,)),
    rs_s=pltpu.SemaphoreType.DMA((12 * 8,)),
    rs_r=pltpu.SemaphoreType.DMA((12 * 8,)),
    a2a_s=pltpu.SemaphoreType.DMA((32,)),
    a2a_r=pltpu.SemaphoreType.DMA((32,)),
    px_s=pltpu.SemaphoreType.DMA((16,)),
    px_r=pltpu.SemaphoreType.DMA((16,)),
    loc=pltpu.SemaphoreType.DMA((8,)),
)


def kernel(wpack, tokens, cot, wproj, o_block, o_in, o_w4, o_wp, o_small, *scratch):
    names = list(SCRATCH)
    r = dict(zip(names, scratch[: len(names)]))
    stages = scratch[len(names) :]
    r["dkv"] = r["sbuf"].at[:, 0 : 2 * HEAD]
    r["dh1"] = r["outp"]
    r["dmid"] = r["part"]
    r["gos"] = r["wor"].at[:, :, :, :, :, 0:HALF]
    r["dqt"] = r["ot"]
    dp, sq = lax.axis_index("dp"), lax.axis_index("seq")
    core = lax.rem(sq, 2)
    me = dict(
        x=lax.div(dp, 2),
        y=lax.div(sq, 4),
        z=lax.rem(lax.div(sq, 2), 2) * 2 + lax.rem(dp, 2),
    )
    j_me = lax.div(sq, 2)
    partner = (dp, sq + 1 - 2 * core)

    peers = [dev(shift(me, a, d), core) for a in "xyz" for d in (1, -1)]
    peers.append(partner)
    for dyy, dzz in ((0, 2), (2, 0), (1, 2), (2, 2), (3, 2)):
        peers.append(dev(shift(shift(me, "y", dyy), "z", dzz), core))
    bar = pltpu.get_barrier_semaphore()
    for t in peers:
        pl.semaphore_signal(bar, inc=1, device_id=t, device_id_type=MESH)
    pl.semaphore_wait(bar, len(peers))

    def pair(src, dst, i):
        return pltpu.make_async_remote_copy(
            src_ref=src,
            dst_ref=dst,
            send_sem=r["px_s"].at[i],
            recv_sem=r["px_r"].at[i],
            device_id=partner,
            device_id_type=MESH,
        )

    mine_rows = pl.ds(pl.multiple_of(core * 128, 128), 128)
    their_rows = pl.ds(pl.multiple_of(128 - core * 128, 128), 128)
    half0 = pl.multiple_of(core * HALF, HALF)
    half1 = pl.multiple_of(HALF - core * HALF, HALF)
    own = (me["x"], lax.rem(me["z"], 2), me["y"], lax.div(me["z"], 2))

    def partner_dev_j(t):
        jj = lax.rem(j_me + t, 8)
        return jj, (dp, jj * 2 + core)

    def a2a(k, t, src, dst, to):
        return pltpu.make_async_remote_copy(
            src_ref=src,
            dst_ref=dst,
            send_sem=r["a2a_s"].at[k * 8 + t],
            recv_sem=r["a2a_r"].at[k * 8 + t],
            device_id=to,
            device_id_type=MESH,
        )

    def tok(jj):
        return pl.ds(pl.multiple_of(jj * T, T), T)

    px_w = pair(wpack.at[1 - core], r["wrecv"], 0)
    px_w.start()
    px_x = pair(tokens, r["x"].at[mine_rows], 1)
    px_x.start()
    px_dy = pair(cot, r["dy"].at[mine_rows], 2)
    px_dy.start()
    lc = [
        pltpu.make_async_copy(tokens, r["x"].at[mine_rows], r["loc"].at[0]),
        pltpu.make_async_copy(cot, r["dy"].at[mine_rows], r["loc"].at[1]),
        pltpu.make_async_copy(wproj, r["wp"].at[own], r["loc"].at[2]),
    ]
    for c in lc:
        c.start()
    px_w.wait_recv()
    mine, theirs = wpack[core], r["wrecv"][...]
    first = jnp.where(core == 0, mine, theirs)
    second = jnp.where(core == 0, theirs, mine)
    r["w4"][own] = jnp.concatenate([first, second], axis=0).astype(BF16)
    lc[2].wait()

    def gathers(table, base):
        out = []
        for i, (name, c0, n, rot) in enumerate(table):
            out.append(Gather(me, core, r[name], c0, n, rot, r["ag_s"], r["ag_r"], (base + i) * 12))
        return out

    ga = gathers(GATHER_A, 0)
    gb = gathers(GATHER_B, len(GATHER_A))
    for ph in range(2):
        for g in ga + gb:
            g.start(ph)
        for g in ga + gb:
            g.forward(ph)
        for g in ga + gb:
            g.finish(ph)
    for g in ga:
        g.start(2)
    for g in ga:
        g.forward(2)
    for g in gb:
        g.start(2)
    lc[0].wait()
    lc[1].wait()
    px_x.wait_recv()
    for g in ga:
        g.finish(2)

    lane = lax.broadcasted_iota(jnp.int32, (8, 128), 1)
    vec_t = [jnp.zeros((8, 128), F32) for _ in range(8)]
    fcb_t = [jnp.zeros((8, 128), F32) for _ in range(16)]
    for p in range(64):
        tile = r["w4"][p // 16, (p // 8) % 2, (p // 2) % 4, p % 2, :, SMALL0 : SMALL0 + 128]
        tile = tile.astype(F32)
        lo, hi = tile[0:8], tile[8:16]
        at = 16 * (p % 8)
        both = jnp.where(lane < 8, lo, 0.0) + pltpu.roll(jnp.where(lane < 8, hi, 0.0), 8, 1)
        vec_t[p // 8] = vec_t[p // 8] + (pltpu.roll(both, at, 1) if at else both)
        fc = jnp.where(core == 0, lo, hi)
        fc = jnp.where((lane >= 32) & (lane < 64), fc, 0.0)
        sh = (32 * (p % 4) - 32) % 128
        fcb_t[p // 4] = fcb_t[p // 4] + (pltpu.roll(fc, sh, 1) if sh else fc)
    for k in range(8):
        r["vec"][:, 128 * k : 128 * k + 128] = vec_t[k]
    for k in range(16):
        r["fcb"][:, 128 * k : 128 * k + 128] = fcb_t[k]

    def vrow(i):
        return r["vec"][i : i + 1, :]

    def ln1(rows, c):
        xhat, _ = norm_stats(r["x"][rows, :].astype(F32))
        r["h1"][rows, :] = (xhat * vrow(0) + vrow(2)).astype(BF16)
        return c

    rows_loop(T, 32, ln1)
    for k in range(3):
        w = r["w4"][:, :, :, :, :, k * HALF : (k + 1) * HALF].reshape(D, HALF)
        v = nn(r["h1"][...], w)
        if k == 0:
            v = v + r["vec"][4:5, pl.ds(half0, HALF)]
        if k == 2:
            v = v + r["vec"][5:6, pl.ds(half0, HALF)]
        r["qkvs"][k] = v.T.astype(BF16).reshape(8, HEAD, T)

    def send_a2a1(start):
        for t in range(1, 8):
            jj, to = partner_dev_j(t)
            c = a2a(0, t, r["qkvs"].at[:, jj], r["qkvt"].at[:, :, tok(j_me)], to)
            c.start() if start else c.wait_send()

    send_a2a1(True)
    r["qkvt"][:, :, tok(j_me)] = r["qkvs"][:, j_me]
    for g in gb:
        g.forward(2)
    for t in range(1, 8):
        jj = lax.rem(j_me + 8 - t, 8)
        a2a(0, t, r["qkvs"].at[:, jj], r["qkvt"].at[:, :, tok(jj)], partner).wait_recv()

    r["qz"][0:HEAD, :] = r["qkvt"][0]
    r["qz"][HEAD:, :] = jnp.zeros((HEAD, LEN), BF16)

    def to_rows(ref, parts):
        def one(i, c):
            cols = pl.ds(pl.multiple_of(i * JB, JB), JB)
            stacked = jnp.concatenate([p(cols) for p in parts], axis=0).astype(F32)
            ref[cols, :] = stacked.T.astype(BF16)
            return c

        lax.fori_loop(0, LEN // JB, one, 0)

    to_rows(r["kv"], [lambda cols: r["qkvt"][1, :, cols], lambda cols: r["qkvt"][2, :, cols]])

    row_i = lax.broadcasted_iota(jnp.int32, (JB, IB), 0)
    col_i = lax.broadcasted_iota(jnp.int32, (JB, IB), 1)

    def jcols(jb):
        return pl.ds(pl.multiple_of(jb * JB, JB), JB)

    def attend(ib, c):
        icols = pl.ds(pl.multiple_of(ib * IB, IB), IB)
        q = r["qz"][:, icols]
        nfull = lax.div(ib * IB, JB)

        def fold_max(s):
            return jnp.max(s.reshape(JB // 8, 8, IB), axis=0)

        def scores(jb, m):
            s = nn(r["kv"][jcols(jb), :], q)
            r["sbuf"][jcols(jb), :] = s
            return jnp.maximum(m, fold_max(s))

        m = lax.fori_loop(0, nfull, scores, jnp.full((8, IB), LOW, F32))
        s = nn(r["kv"][jcols(nfull), :], q)
        s = jnp.where(nfull * JB + row_i <= ib * IB + col_i, s, LOW)
        r["sbuf"][jcols(nfull), :] = s
        m = jnp.max(jnp.maximum(m, fold_max(s)), axis=0, keepdims=True) * SCALE2

        def weigh(jb, state):
            l, o = state
            p = jnp.exp2(r["sbuf"][jcols(jb), :] * SCALE2 - m)
            l = l + fold8(p)
            return l, o + nn(r["qkvt"][2, :, jcols(jb)], p.astype(BF16))

        l, o = lax.fori_loop(
            0, nfull + 1, weigh, (jnp.zeros((8, IB), F32), jnp.zeros((HEAD, IB), F32))
        )
        l = jnp.sum(l, axis=0, keepdims=True)
        o = o / l
        r["ot"][:, icols] = o
        r["ots"][:, icols] = o.astype(BF16)
        r["lse"][:, icols] = jnp.broadcast_to(m + jnp.log2(l), (8, IB))
        return c

    lax.fori_loop(0, LEN // IB, attend, 0)

    def send_a2a2(start):
        for t in range(1, 8):
            jj, to = partner_dev_j(t)
            c = a2a(1, t, r["ots"].at[:, tok(jj)], r["attt"].at[j_me], to)
            c.start() if start else c.wait_send()

    send_a2a2(True)
    r["attt"][j_me] = r["ots"][:, tok(j_me)]

    for g in gb:
        g.finish(2)
    keep = r["w4"].at[pl.ds(2 * core, 2), :, :, :, :, pl.ds(OUT0, HALF)]
    give = r["w4"].at[pl.ds(2 - 2 * core, 2), :, :, :, :, pl.ds(OUT0, HALF)]
    wor_mine = r["wor"].at[:, :, :, :, :, pl.ds(half0, HALF)]
    px_wo = pair(give, wor_mine, 3)
    px_wo.start()
    lc_wo = pltpu.make_async_copy(keep, wor_mine, r["loc"].at[3])
    lc_wo.start()
    for t in range(1, 8):
        jj = lax.rem(j_me + 8 - t, 8)
        a2a(1, t, r["ots"].at[:, tok(jj)], r["attt"].at[jj], partner).wait_recv()
    lc_wo.wait()
    px_wo.wait_recv()

    att = r["attt"][...].reshape(8 * HEAD, T).astype(F32).T.astype(BF16)
    r["part"][...] = nn(att, r["wor"][...].reshape(HALF, D))
    px_p = pair(r["part"], r["partr"], 4)
    px_p.start()
    px_p.wait()

    def ln2(rows, c):
        mid = r["x"][rows, :].astype(F32) + (r["part"][rows, :] + r["partr"][rows, :] + vrow(6))
        r["middle"][rows, :] = mid
        xhat, _ = norm_stats(mid)
        r["h2"][rows, :] = (xhat * vrow(1) + vrow(3)).astype(BF16)
        return c

    rows_loop(T, 32, ln2)
    r["h2t"][...] = r["h2"][...].astype(F32).T.astype(BF16)
    r["outp"][...] = jnp.zeros((T, D), F32)
    r["dh"][...] = jnp.zeros((T, D), F32)
    px_dy.wait_recv()

    def ffn(t, c):
        hi, lo = lax.div(t, 2), lax.rem(t, 2)
        cols = pl.ds(pl.multiple_of(t * 256, 256), 256)
        wf = r["w4"][:, :, :, :, :, pl.ds(pl.multiple_of(FC0 + t * 256, 128), 256)].reshape(D, 256)
        wp = r["wp"][hi, lo].reshape(256, D)
        pre = nn(r["h2"][...], wf) + r["fcb"][0:1, cols]
        d_act = nt(r["dy"][...], wp)
        sq_ = pre * pre
        th = jnp.tanh(0.7978845608028654 * (pre + 0.044715 * sq_ * pre))
        act = 0.5 * pre * (1.0 + th)
        slope = 0.5 * (1.0 + th) + 0.5 * pre * (1.0 - th * th) * (
            0.7978845608028654 * (1.0 + 3.0 * 0.044715 * sq_)
        )
        d_pre = (slope * d_act).astype(BF16)
        r["outp"][...] += nn(act.astype(BF16), wp)
        r["gp"][hi, lo] = (
            nn(act.T.astype(BF16), r["dy"][...]).astype(BF16).reshape(4, 2, 32, D)
        )
        r["g4"][:, :, :, :, :, pl.ds(pl.multiple_of(GFC0 + t * 256, 256), 256)] = (
            nn(r["h2t"][...], d_pre).astype(BF16).reshape(4, 2, 4, 2, 16, 256)
        )
        r["sfc"][:, cols] = jnp.broadcast_to(
            jnp.sum(d_pre.astype(F32), axis=0, keepdims=True), (8, 256)
        )
        r["dh"][...] += nt(d_pre, wf)
        return c

    lax.fori_loop(0, 8, ffn, 0)

    px_dh = pair(r["dh"], r["dhr"], 5)
    px_dh.start()
    px_out = pair(r["outp"].at[their_rows], r["outr"], 6)
    px_out.start()

    def reduces(table, base, stage_at):
        out = []
        for i, (name, c0, n, rot) in enumerate(table):
            piece = Reduce(me, core, r[name], c0, n, rot, r["rs_s"], r["rs_r"], (base + i) * 12)
            k = (stage_at + i) * 9
            out.append(piece.attach(stages[k : k + 9]))
        return out

    rf = reduces(REDUCE_F, 0, 0)
    rq = reduces(REDUCE_Q, len(REDUCE_F), len(REDUCE_F))
    for g in rf:
        g.start(0)

    r["sv"][...] = jnp.zeros((8, D), F32)
    px_dh.wait_recv()

    def ln2_back(rows, c):
        dh = r["dh"][rows, :] + r["dhr"][rows, :]
        r["dhr"][rows, :] = dh
        xhat, inv = norm_stats(r["middle"][rows, :])
        d_mid = r["dy"][rows, :].astype(F32) + norm_back(xhat, inv, dh, vrow(1))
        r["dmid"][rows, :] = d_mid
        r["dbr"][rows, :] = d_mid.astype(BF16)
        return c

    rows_loop(T, 32, ln2_back)

    wor = r["wor"][...].reshape(HALF, D)
    r["datt"][...] = nt(wor, r["dbr"][...]).astype(BF16).reshape(8, HEAD, T)

    def send_a2a3(start):
        for t in range(1, 8):
            jj, to = partner_dev_j(t)
            c = a2a(2, t, r["datt"].at[jj], r["dz"].at[pl.ds(HEAD, HEAD), tok(j_me)], to)
            c.start() if start else c.wait_send()

    send_a2a3(True)
    r["dz"][HEAD:, tok(j_me)] = r["datt"][j_me]
    r["dz"][0:HEAD, :] = jnp.zeros((HEAD, LEN), BF16)

    gout = nn(r["attt"][...].reshape(HALF, T), r["dbr"][...]).astype(BF16)
    left = gout[:, :HALF].reshape(2, 2, 4, 2, 16, HALF)
    right = gout[:, HALF:].reshape(2, 2, 4, 2, 16, HALF)
    go_at = r["g4"].at[pl.ds(2 * core, 2), :, :, :, :, pl.ds(GOUT0, HALF)]
    go_at[...] = jnp.where(core == 0, left, right)
    r["gos"][...] = jnp.where(core == 0, right, left)
    px_go = pair(r["gos"], go_at, 7)
    px_go.start()

    def small2(i, c):
        s1, s2, s3, s4 = c
        rows = pl.ds(pl.multiple_of(core * 128 + i * 32, 32), 32)
        dh = r["dhr"][rows, :]
        xhat, _ = norm_stats(r["middle"][rows, :])
        return (
            s1 + fold8(dh * xhat),
            s2 + fold8(dh),
            s3 + fold8(r["dbr"][rows, :].astype(F32)),
            s4 + fold8(r["dy"][rows, :].astype(F32)),
        )

    zero = jnp.zeros((8, D), F32)
    sums = lax.fori_loop(0, 4, small2, (zero, zero, zero, zero))
    for row, s in zip((1, 3, 6, 7), sums):
        r["sv"][row : row + 1, :] = jnp.sum(s, axis=0, keepdims=True)

    px_out.wait_recv()

    def block_out(i, c):
        rows = pl.ds(pl.multiple_of(core * 128 + i * 32, 32), 32)
        here = pl.ds(pl.multiple_of(i * 32, 32), 32)
        o_block[here, :] = (
            r["middle"][rows, :] + (r["outp"][rows, :] + r["outr"][here, :]) + vrow(7)
        ).astype(BF16)
        return c

    lax.fori_loop(0, 4, block_out, 0)
    px_out.wait_send()

    for g in rf:
        g.forward(0)

    for t in range(1, 8):
        jj = lax.rem(j_me + 8 - t, 8)
        a2a(2, t, r["datt"].at[jj], r["dz"].at[pl.ds(HEAD, HEAD), tok(jj)], partner).wait_recv()

    to_rows(r["qd"], [lambda cols: r["qz"][0:HEAD, cols], lambda cols: r["dz"][HEAD:, cols]])
    r["rowdot"][...] = jnp.broadcast_to(
        jnp.sum(r["dz"][HEAD:, :].astype(F32) * r["ot"][...], axis=0, keepdims=True), (8, LEN)
    )
    r["dkv"][...] = jnp.zeros((LEN, 2 * HEAD), F32)
    lane_kv = lax.broadcasted_iota(jnp.int32, (JB, 2 * HEAD), 1)

    def attend_back(ib, c):
        icols = pl.ds(pl.multiple_of(ib * IB, IB), IB)
        q, do = r["qz"][:, icols], r["dz"][:, icols]
        qd = r["qd"][icols, :]
        lse, dot = r["lse"][0:1, icols], r["rowdot"][0:1, icols]
        nfull = lax.div(ib * IB, JB)

        def step(jb, dq, masked):
            kv = r["kv"][jcols(jb), :]
            p = jnp.exp2(nn(kv, q) * SCALE2 - lse)
            if masked:
                p = jnp.where(jb * JB + row_i <= ib * IB + col_i, p, 0.0)
            ds = (p * (nn(kv, do) - dot)).astype(BF16)
            r["dkv"][jcols(jb), :] += jnp.where(
                lane_kv < HEAD, nn(ds, qd), nn(p.astype(BF16), qd)
            )
            return dq + nn(r["qkvt"][1, :, jcols(jb)], ds)

        dq = lax.fori_loop(
            0, nfull, lambda jb, a: step(jb, a, False), jnp.zeros((HEAD, IB), F32)
        )
        r["dqt"][:, icols] = step(nfull, dq, True)

        @pl.when(ib == 3)
        def _():
            for g in rf:
                g.finish(0)
            for g in rf:
                g.start(1)

        @pl.when(ib == 5)
        def _():
            for g in rf:
                g.forward(1)

        return c

    lax.fori_loop(0, LEN // IB, attend_back, 0)

    r["dqkvt"][0] = (r["dqt"][...] * 0.125).astype(BF16)

    def kv_back(jb, c):
        both = r["dkv"][jcols(jb), :].T
        r["dqkvt"][1, :, jcols(jb)] = (both[:HEAD] * 0.125).astype(BF16)
        r["dqkvt"][2, :, jcols(jb)] = both[HEAD:].astype(BF16)
        return c

    lax.fori_loop(0, LEN // JB, kv_back, 0)

    def send_a2a4(start):
        for t in range(1, 8):
            jj, to = partner_dev_j(t)
            c = a2a(3, t, r["dqkvt"].at[:, :, tok(jj)], r["dqs"].at[:, j_me], to)
            c.start() if start else c.wait_send()

    send_a2a4(True)
    r["dqs"][:, j_me] = r["dqkvt"][:, :, tok(j_me)]
    for g in rf:
        g.finish(1)
    for g in rf:
        g.start(2)
    for t in range(1, 8):
        jj = lax.rem(j_me + 8 - t, 8)
        a2a(3, t, r["dqkvt"].at[:, :, tok(jj)], r["dqs"].at[:, jj], partner).wait_recv()

    h1t = r["h1"][...].astype(F32).T.astype(BF16)
    for k in range(3):
        dt = r["dqs"][k].reshape(HALF, T)
        r["g4"][:, :, :, :, :, k * HALF : (k + 1) * HALF] = (
            nt(h1t, dt).astype(BF16).reshape(4, 2, 4, 2, 16, HALF)
        )
    px_go.wait_recv()
    for g in rq[:3]:
        g.start(0)
    for k in range(3):
        d = r["dqs"][k].reshape(HALF, T).astype(F32).T
        if k != 1:
            row = 4 if k == 0 else 5
            r["sv"][row : row + 1, pl.ds(half0, HALF)] = jnp.sum(d, axis=0, keepdims=True)
        w = r["w4"][:, :, :, :, :, k * HALF : (k + 1) * HALF].reshape(D, HALF)
        v = nt(d.astype(BF16), w)
        r["dh1"][...] = v if k == 0 else r["dh1"][...] + v
    px_d1 = pair(r["dh1"].at[their_rows], r["dh1r"], 8)
    px_d1.start()
    for g in rf:
        g.forward(2)
    px_d1.wait_recv()

    def ln1_back(i, c):
        s1, s2 = c
        rows = pl.ds(pl.multiple_of(core * 128 + i * 32, 32), 32)
        here = pl.ds(pl.multiple_of(i * 32, 32), 32)
        dh = r["dh1"][rows, :] + r["dh1r"][here, :]
        xhat, inv = norm_stats(r["x"][rows, :].astype(F32))
        d_in = r["dmid"][rows, :] + norm_back(xhat, inv, dh, vrow(0))
        o_in[here, :] = d_in.astype(BF16)
        return s1 + fold8(dh * xhat), s2 + fold8(dh)

    sums = lax.fori_loop(0, 4, ln1_back, (zero, zero))
    for row, s in zip((0, 2), sums):
        r["sv"][row : row + 1, :] = jnp.sum(s, axis=0, keepdims=True)

    for p in range(64):
        k, at = p // 8, 16 * (p % 8)
        v = r["sv"][:, 128 * k : 128 * k + 128]
        v = pltpu.roll(v, (128 - at) % 128, 1) if at else v
        k, sh = p // 4, (32 - 32 * (p % 4)) % 128
        f = r["sfc"][:, 128 * k : 128 * k + 128]
        f = pltpu.roll(f, sh, 1) if sh else f
        r["gs"][p // 16, (p // 8) % 2, (p // 2) % 4, p % 2] = jnp.where(
            lane < 16, v, jnp.where((lane >= 32) & (lane < 64), f, 0.0)
        )
    rq[3].start(0)

    def out_of(g, wide, tall):
        return wide.at[:, pl.ds(g.c0, g.n)] if tall is None else tall.at[:, pl.ds(g.c0, g.n)]

    for ph in range(3):
        for g in rq:
            g.forward(ph)
        if ph == 0:
            for g in rf:
                g.finish(2, out_of(g, r["fin"], o_wp if g.ref is r["gp"] else None))
        for i, g in enumerate(rq):
            out = None
            if ph == 2:
                out = r["fins"] if i == 3 else out_of(g, r["fin"], None)
            g.finish(ph, out)
            if ph < 2:
                g.start(ph + 1)

    mine8 = pl.ds(pl.multiple_of(core * 8, 8), 8)
    their8 = pl.ds(pl.multiple_of(8 - core * 8, 8), 8)
    px_f = pair(r["fin"].at[their8], o_w4.at[core], 9)
    px_f.start()
    px_s = pair(r["fins"], r["finr"], 10)
    px_s.start()
    o_w4[core] = r["fin"][mine8, :]
    px_f.wait_recv()
    px_s.wait_recv()
    total = r["fins"][...] + jnp.where(lane < 16, r["finr"][...], 0.0)
    shifted = jnp.where(core == 0, total, pltpu.roll(total, 120, 1))
    o_small[...] = jnp.where(lane < 8, shifted, total)

    for g in ga + gb + rf + rq:
        g.drain()
    for c in (px_w, px_x, px_dy, px_wo, px_dh, px_go, px_d1, px_f, px_s):
        c.wait_send()
    send_a2a1(False)
    send_a2a2(False)
    send_a2a3(False)
    send_a2a4(False)


def stage_list():
    out = []
    for name, _, n, rot in REDUCE_F + REDUCE_Q:
        out += Reduce.stage_shapes(ROWS[name], n, rot, TYPES[name])
    return out


def block(wpack, tokens, cot, wproj):
    vm = pl.BlockSpec(memory_space=pltpu.VMEM)
    return pl.pallas_call(
        kernel,
        out_shape=(
            jax.ShapeDtypeStruct((128, D), BF16),
            jax.ShapeDtypeStruct((128, D), BF16),
            jax.ShapeDtypeStruct((2, 8, G4), F32),
            jax.ShapeDtypeStruct((32, D), F32),
            jax.ShapeDtypeStruct((8, 128), F32),
        ),
        in_specs=[vm] * 4,
        out_specs=(vm,) * 5,
        scratch_shapes=list(SCRATCH.values()) + stage_list(),
        compiler_params=pltpu.CompilerParams(
            collective_id=0, has_side_effects=True, vmem_limit_bytes=63 * 2**20
        ),
    )(wpack, tokens, cot, wproj)


def on_device(
    tokens,
    norm_gains,
    norm_biases,
    w_qkv,
    attn_biases,
    w_out,
    branch_biases,
    w_fc,
    fc_bias,
    w_proj,
    cotangent,
):
    q = w_qkv.reshape(8, 3, 2, HALF).transpose(2, 0, 1, 3).reshape(2, 8, 3 * HALF)
    o = w_out.reshape(8, 2, HALF).transpose(1, 0, 2)
    f = w_fc.reshape(8, 64, 2, 32).transpose(2, 0, 1, 3).reshape(2, 8, FFH)
    vectors = jnp.concatenate([norm_gains, norm_biases, attn_biases, branch_biases], axis=0)
    fcb = jnp.concatenate([fc_bias[None], jnp.zeros((7, 32), BF16)], axis=0)
    small = jnp.concatenate(
        [vectors, jnp.zeros((8, 24), BF16), fcb, jnp.zeros((8, 64), BF16)], axis=1
    )
    small = jnp.broadcast_to(small[None], (2, 8, 128))
    wpack = jnp.concatenate([q, small, o, f], axis=2).astype(F32)
    block_out, input_grad, gw4, gwp, gsmall = block(wpack, tokens[0], cotangent[0], w_proj)
    gq = gw4[:, :, :GOUT0].reshape(2, 8, 3, HALF).transpose(1, 2, 0, 3).reshape(8, 3 * D)
    go = gw4[:, :, GOUT0:GFC0].transpose(1, 0, 2).reshape(8, D)
    gf = gw4[:, :, GFC0:].reshape(2, 8, 64, 32).transpose(1, 2, 0, 3).reshape(8, FF)
    return (
        block_out[None],
        input_grad[None],
        gsmall[0:2, :8],
        gsmall[2:4, :8],
        gq,
        gsmall[4:6, :8],
        go,
        gsmall[6:8, :8],
        gf,
        gsmall[0, 32:64],
        gwp,
    )


def solution(mesh):
    in_specs = (
        P("dp", "seq", None),
        P(None, ("dp", "seq")),
        P(None, ("dp", "seq")),
        P(("dp", "seq"), None),
        P(None, ("dp", "seq")),
        P(("dp", "seq"), None),
        P(None, ("dp", "seq")),
        P(("dp", "seq"), None),
        P(("dp", "seq")),
        P(("dp", "seq"), None),
        P("dp", "seq", None),
    )
    out_specs = (
        P("dp", "seq", None),
        P("dp", "seq", None),
        P(None, ("dp", "seq")),
        P(None, ("dp", "seq")),
        P(("dp", "seq"), None),
        P(None, ("dp", "seq")),
        P(("dp", "seq"), None),
        P(None, ("dp", "seq")),
        P(("dp", "seq"), None),
        P(("dp", "seq")),
        P(("dp", "seq"), None),
    )
    return jax.shard_map(
        on_device, mesh=mesh, in_specs=in_specs, out_specs=out_specs, check_vma=False
    )
```

time: 4130 us -> 207 us (0.05)
  waiting for transfers between devices: 3150 us -> 0 us
  blocking collectives: 831 us -> 0 us
  Pallas kernels: 0 us -> 192 us
  matrix products: 76.3 us -> 0 us
    reduce_scatter x4 -> x0, waiting for transfers between devices: 2530 us -> none  [the longest x1 671 us: on_device(): lax.psum_scatter(g_fc, ('dp', 'seq'), scatter_dimension=0, tiled=True)]
    all_gather x4 -> x0, blocking collectives: 696 us -> none  [the longest x1 180 us: on_device(): lax.all_gather(norm_gains, ('dp', 'seq'), axis=1, tiled=True)]
    all_gather x6 -> x0, waiting for transfers between devices: 435 us -> none  [the longest x1 201 us: on_device(): lax.all_gather(w_fc, ('dp', 'seq'), axis=0, tiled=True)]
    pallas_call x0 -> x1, Pallas kernels: none -> 192 us  [block(): pl.pallas_call(kernel, out_shape=(jax.ShapeDtypeStruct((128, D), BF16), j...]
    unnamed x14 -> x0, waiting for transfers between devices: 183 us -> none
    unnamed x2 -> x0, blocking collectives: 135 us -> none
    dot_general x19 -> x0, matrix products: 76.3 us -> none  [the longest x1 9.7 us: on_device(): g_proj = jnp.dot(act.T, grad_out, preferred_element_type=jnp.float32)]
  transfers between devices with their start and end apart: 12 -> 0, of which waited for: 9 -> 0; matrix products, arithmetic and copies ran while one was open for 2% -> 0% of each run, Pallas kernels for 0% -> 0%
where the time goes in v1:
time: 207 us; the launch traced here: 206 us
  Pallas kernels  192 us (93%)
  local copies, waits for them, and re-layouts  12.1 us (6%)
    pallas_call x1, Pallas kernels, block(): pl.pallas_call(kernel, out_shape=(jax.ShapeDtypeStruct((128, D), BF16), j...  192 us

profile of v1, /device:TPU:1, one launch (start us, length us, event | category | flops | bytes accessed | tf_op | source)
XLA Modules:
  0.0 206.4 jit_solution(7463353500176943653)
XLA Ops:
  0.6 0.0 copy-start.4
  0.7 0.1 pad.11.clone
  0.7 0.1 pad.9.clone
  0.8 0.8 fusion.3
  1.6 0.8 copy.26
  2.4 0.0 copy-done.4
  2.4 0.2 reshape.56
  2.7 0.0 copy-start.5
  2.7 0.3 reshape.57
  3.0 0.4 copy-done.5
  3.4 0.7 maximum_convert_fusion.wpack
  4.1 192.0 %shard_map.194 = (bf16[128,1024]{1,0:T(8,128)(2,1)}, bf16[128,1024]{1,0:T(8,128)(2,1)}, f32[2,8,4096]{2,1,0:T(8,128)}, f32[32,1024]{1,0:T(8,128)}, f32[8,128]{1,0:T(8,128)}) custom-call(f32[2,8,4224]{2,1,0:T(8,128)} %maximum_convert_fusion.wpack, bf16[128,1024]{1,0:T(8,128)(2,1)} %bitcast.28, bf16[128,1024]{1,0:T(8,128)(2,1)} %bitcast.29, bf16[32,1024]{1,0:T(8,128)(2,1)} %wproj.1), custom_call_target="tpu_custom_call" | custom-call | tf_op jit(solution)/shard_map/pallas_call | solution.py:882
  196.1 0.0 copy-start.2
  196.2 1.3 slice_bitcast_fusion
  197.5 1.4 fusion.4
  198.9 1.4 slice.28
  200.2 0.9 slice.26
  201.1 0.0 copy-done.2
  201.2 0.6 copy.28
  201.8 0.2 reshape.61
  202.0 0.4 copy.29
  202.4 0.0 copy-start.1
  202.4 1.3 reshape.62
  203.7 0.0 copy-done.1
  203.7 0.0 copy-start
  203.7 0.7 copy.33
  204.4 0.3 copy-done
  204.8 0.0 copy-start.3
  204.8 0.7 copy.34
  205.5 0.3 copy-done.3
  205.8 0.7 copy.35
  (5 shorter events, 0.1 us)
Async XLA Ops:
  0.6 1.8 copy-start.4
  2.7 0.7 copy-start.5
  196.1 5.0 %copy-start.2 = (f32[2,8,4096]{2,1,0:T(8,128)S(1)}, f32[2,8,4096]{2,1,0:T(8,128)}, u32[]{:S(2)}) copy-start(f32[2,8,4096]{2,1,0:T(8,128)} %get-tuple-element.19) | copy-start | bytes 786436
  202.4 1.3 copy-start.1
  203.7 1.0 copy-start
  204.8 1.0 copy-start.3

commit v2 on v1

--- a/solution.py
+++ b/solution.py
@@ -28,8 +28,8 @@
 OUT0 = SMALL0 + 128
 FC0 = OUT0 + HALF
 W4 = FC0 + FFH
-GOUT0 = 3 * HALF
-GFC0 = GOUT0 + HALF
+GOUT0 = 0
+GFC0 = HALF
 G4 = GFC0 + FFH
 
 JB = 512
@@ -97,11 +97,25 @@
     return 0 if d > 0 else 1
 
 
+def remote_copy(src, dst, sems, i, to):
+    return pltpu.make_async_remote_copy(
+        src_ref=src,
+        dst_ref=dst,
+        send_sem=sems[0].at[i],
+        recv_sem=sems[1].at[i],
+        device_id=to,
+        device_id_type=MESH,
+    )
+
+
+ring_copy = remote_copy
+
+
 class Piece:
-    def __init__(self, me, core, ref, c0, n, rot, ssem, rsem, base):
+    def __init__(self, me, core, ref, c0, n, rot, sems, base):
         self.me, self.core, self.ref, self.c0, self.n = me, core, ref, c0, n
         self.order = ORDERS[rot]
-        self.ssem, self.rsem, self.base = ssem, rsem, base
+        self.sems, self.base = sems, base
 
     def cols(self, h):
         if h is None:
@@ -110,18 +124,8 @@
         return self.c0 + off, n
 
     def remote(self, src, dst, ph, st, d):
-        i = self.base + ph * 4 + st * 2 + way(d)
-        return pltpu.make_async_remote_copy(
-            src_ref=src,
-            dst_ref=dst,
-            send_sem=self.ssem.at[i],
-            recv_sem=self.rsem.at[i],
-            device_id=dev(shift(self.me, self.order[ph], d), self.core),
-            device_id_type=MESH,
-        )
-
-    def ways(self, st):
-        return (1, -1)
+        to = dev(shift(self.me, self.order[ph], d), self.core)
+        return ring_copy(src, dst, self.sems, self.base + ph * 4 + st * 2 + way(d), to)
 
 
 class Gather(Piece):
@@ -131,6 +135,9 @@
             sel[a] = None if k < ph else (mod4(self.me[a] + off) if k == ph else self.me[a])
         return blocks(self.ref, sel, *self.cols(h))
 
+    def ways1(self):
+        return (1, -1) if self.n > 128 else (1,)
+
     def copy(self, ph, st, d):
         r = self.region(ph, 0, None) if st == 0 else self.region(ph, -d, way(d))
         return self.remote(r, r, ph, st, d)
@@ -143,18 +150,20 @@
         for d in (1, -1):
             r = self.region(ph, -d, None)
             self.remote(r, r, ph, 0, d).wait_recv()
-            self.copy(ph, 1, d).start()
+            if d in self.ways1():
+                self.copy(ph, 1, d).start()
 
     def finish(self, ph):
-        for d in (1, -1):
+        for d in self.ways1():
             r = self.region(ph, -2 * d, way(d))
             self.remote(r, r, ph, 1, d).wait_recv()
 
     def drain(self):
         for ph in range(3):
-            for st in range(2):
-                for d in (1, -1):
-                    self.copy(ph, st, d).wait_send()
+            for d in (1, -1):
+                self.copy(ph, 0, d).wait_send()
+            for d in self.ways1():
+                self.copy(ph, 1, d).wait_send()
 
 
 class Reduce(Piece):
@@ -193,10 +202,10 @@
 
     def add(self, target, sources, lead):
         def one(idx):
-            total = target[idx].astype(F32)
+            total = target[idx]
             for s in sources:
-                total = total + s[idx].astype(F32)
-            target[idx] = total.astype(target.dtype)
+                total = total + s[idx]
+            target[idx] = total
 
         if not lead:
             one(Ellipsis)
@@ -230,22 +239,27 @@
                 self.copy(ph, 1, d).wait_send()
 
 
+GATHER_B = (
+    ("w4", OUT0, HALF + 256, 0),
+    ("w4", FC0 + 256, 768, 1),
+    ("w4", FC0 + 1024, 768, 2),
+)
+GATHER_C = (
+    ("w4", FC0 + 1792, 256, 0),
+    ("wp", 0, 256, 0),
+    ("wp", 256, 384, 1),
+    ("wp", 640, 384, 2),
+)
 GATHER_A = (("w4", 0, HALF, 0), ("w4", HALF, HALF, 1), ("w4", 2 * HALF, HALF + 128, 2))
-GATHER_B = (
-    ("w4", OUT0, HALF + 1024, 0),
-    ("w4", FC0 + 1024, 1024, 1),
-    ("wp", 768, 256, 1),
-    ("wp", 0, 768, 2),
+REDUCE_P = (("gp", 0, HALF, 1), ("gp", HALF, HALF, 2))
+REDUCE_F = (
+    ("g4", GFC0, 640, 0),
+    ("g4", GFC0 + 640, 640, 0),
+    ("g4", GFC0 + 1280, 256, 1),
+    ("g4", GFC0 + 1536, HALF, 2),
 )
-REDUCE_F = (
-    ("g4", GFC0, 1280, 0),
-    ("g4", GFC0 + 1280, 768, 1),
-    ("gp", 0, 256, 1),
-    ("gp", 256, 768, 2),
-)
-REDUCE_Q = (("g4", 0, 640, 0), ("g4", 640, 640, 1), ("g4", 1280, 768, 2), ("gs", 0, 128, 0))
-ROWS = {"g4": 16, "gp": 32, "gs": 8}
-TYPES = {"g4": BF16, "gp": BF16, "gs": F32}
+REDUCE_O = (("g4", GOUT0, HALF, 0),)
+ROWS = {"g4": 16, "gp": 32}
 
 
 def rows_loop(total, step, body, init=0):
@@ -279,18 +293,20 @@
     wp=pltpu.VMEM((4, 2, 4, 2, 32, D), BF16),
     g4=pltpu.VMEM((4, 2, 4, 2, 16, G4), BF16),
     gp=pltpu.VMEM((4, 2, 4, 2, 32, D), BF16),
-    gs=pltpu.VMEM((4, 2, 4, 2, 8, 128), F32),
+    pack=pltpu.VMEM((2, 8, W4), F32),
+    tiny=pltpu.VMEM((2, 8, 128), F32),
     wrecv=pltpu.VMEM((8, W4), F32),
     wor=pltpu.VMEM((2, 2, 4, 2, 16, D), BF16),
+    hs=pltpu.VMEM((4, 2, 2, 128, D), BF16),
+    h1=pltpu.VMEM((T, D), BF16),
+    qkvs=pltpu.VMEM((3, 8, HEAD, T), BF16),
+    qkvt=pltpu.VMEM((3, HEAD, LEN), BF16),
     x=pltpu.VMEM((T, D), BF16),
     dy=pltpu.VMEM((T, D), BF16),
-    h1=pltpu.VMEM((T, D), BF16),
     h2=pltpu.VMEM((T, D), BF16),
     h2t=pltpu.VMEM((D, T), BF16),
     vec=pltpu.VMEM((8, D), F32),
     fcb=pltpu.VMEM((8, FFH), F32),
-    qkvs=pltpu.VMEM((3, 8, HEAD, T), BF16),
-    qkvt=pltpu.VMEM((3, HEAD, LEN), BF16),
     qz=pltpu.VMEM((2 * HEAD, LEN), BF16),
     dz=pltpu.VMEM((2 * HEAD, LEN), BF16),
     kv=pltpu.VMEM((LEN, 2 * HEAD), BF16),
@@ -301,6 +317,8 @@
     lse=pltpu.VMEM((8, LEN), F32),
     rowdot=pltpu.VMEM((8, LEN), F32),
     attt=pltpu.VMEM((8, HEAD, T), BF16),
+    act=pltpu.VMEM((T, FFH), BF16),
+    dpre=pltpu.VMEM((T, FFH), BF16),
     part=pltpu.VMEM((T, D), F32),
     partr=pltpu.VMEM((T, D), F32),
     middle=pltpu.VMEM((T, D), F32),
@@ -313,26 +331,125 @@
     dqkvt=pltpu.VMEM((3, HEAD, LEN), BF16),
     dqs=pltpu.VMEM((3, 8, HEAD, T), BF16),
     dh1r=pltpu.VMEM((T // 2, D), F32),
+    gqs=pltpu.VMEM((8, 3 * HEAD, 128), BF16),
+    gqr=pltpu.VMEM((8, 3 * HEAD, 128), BF16),
+    gqt=pltpu.VMEM((8, 16, 256), F32),
+    finq=pltpu.VMEM((8, 16, 256), F32),
     sv=pltpu.VMEM((8, D), F32),
     sfc=pltpu.VMEM((8, FFH), F32),
+    ss=pltpu.VMEM((8, 16, 128), F32),
+    ssr=pltpu.VMEM((8, 16, 128), F32),
+    st=pltpu.VMEM((16, 128), F32),
+    str=pltpu.VMEM((8, 16, 128), F32),
     fin=pltpu.VMEM((16, G4), F32),
-    fins=pltpu.VMEM((8, 128), F32),
-    finr=pltpu.VMEM((8, 128), F32),
-    ag_s=pltpu.SemaphoreType.DMA((12 * 7,)),
-    ag_r=pltpu.SemaphoreType.DMA((12 * 7,)),
-    rs_s=pltpu.SemaphoreType.DMA((12 * 8,)),
-    rs_r=pltpu.SemaphoreType.DMA((12 * 8,)),
-    a2a_s=pltpu.SemaphoreType.DMA((32,)),
-    a2a_r=pltpu.SemaphoreType.DMA((32,)),
+    fins=pltpu.VMEM((16, 128), F32),
+    finr=pltpu.VMEM((16, 128), F32),
+    ag_s=pltpu.SemaphoreType.DMA((12 * 10,)),
+    ag_r=pltpu.SemaphoreType.DMA((12 * 10,)),
+    rs_s=pltpu.SemaphoreType.DMA((12 * 7,)),
+    rs_r=pltpu.SemaphoreType.DMA((12 * 7,)),
+    xg_s=pltpu.SemaphoreType.DMA((6,)),
+    xg_r=pltpu.SemaphoreType.DMA((6,)),
+    a2a_s=pltpu.SemaphoreType.DMA((48,)),
+    a2a_r=pltpu.SemaphoreType.DMA((48,)),
+    dp_s=pltpu.SemaphoreType.DMA((24,)),
+    dp_r=pltpu.SemaphoreType.DMA((24,)),
     px_s=pltpu.SemaphoreType.DMA((16,)),
     px_r=pltpu.SemaphoreType.DMA((16,)),
     loc=pltpu.SemaphoreType.DMA((8,)),
 )
 
 
-def kernel(wpack, tokens, cot, wproj, o_block, o_in, o_w4, o_wp, o_small, *scratch):
+def roll(v, shift):
+    shift %= 128
+    return pltpu.roll(v, shift, 1) if shift else v
+
+
+def quarters(pieces):
+    lane = lax.broadcasted_iota(jnp.int32, (8, 128), 1)
+    low = jnp.where(lane < 32, pieces[0], pieces[1])
+    high = jnp.where(lane < 96, pieces[2], pieces[3])
+    return jnp.where(lane < 64, low, high)
+
+
+def pack(pack_ref, tiny, w_qkv, w_out, w_fc, vectors, fc_bias):
+    q, o, f = w_qkv[...].astype(F32), w_out[...].astype(F32), w_fc[...].astype(F32)
+    lane = lax.broadcasted_iota(jnp.int32, (8, 128), 1)
+    tiny[...] = jnp.zeros((2, 8, 128), F32)
+    for i, v in enumerate(vectors):
+        tiny[0, 2 * i : 2 * i + 2, 0:8] = v[...].astype(F32)
+    tiny[1, 0:1, 0:32] = fc_bias[...].astype(F32)
+    small = jnp.where(lane < 8, tiny[0], roll(tiny[1], 32))
+    for h in range(2):
+        for k in range(3):
+            c = k * D + h * HALF
+            pack_ref[h, :, k * HALF : (k + 1) * HALF] = q[:, c : c + HALF]
+        pack_ref[h, :, SMALL0 : SMALL0 + 128] = small
+        pack_ref[h, :, OUT0 : OUT0 + HALF] = o[:, h * HALF : (h + 1) * HALF]
+        for m in range(16):
+            first = f[:, 256 * m : 256 * m + 128]
+            second = f[:, 256 * m + 128 : 256 * m + 256]
+            pack_ref[h, :, FC0 + 128 * m : FC0 + 128 * m + 128] = quarters(
+                [
+                    roll(first, -32 * h),
+                    roll(first, -32 - 32 * h),
+                    roll(second, 64 - 32 * h),
+                    roll(second, 32 - 32 * h),
+                ]
+            )
+
+
+def unpack(block, grad_in, w4, wq, wp, small, *outs):
+    o_block, o_in, o_gains, o_shifts, o_qkv, o_attn, o_out, o_branch, o_fc, o_fcb, o_proj = outs
+    o_block[...] = block[...]
+    o_in[...] = grad_in[...]
+    o_proj[...] = wp[...]
+    for i, o in enumerate((o_gains, o_shifts, o_attn, o_branch)):
+        o[...] = small[2 * i : 2 * i + 2, 0:8]
+    o_fcb[...] = roll(small[...], -32)[0:1, 0:32]
+    lane = lax.broadcasted_iota(jnp.int32, (8, 128), 1)
+    for h in range(2):
+        o_out[:, h * HALF : (h + 1) * HALF] = w4[h, :, GOUT0 : GOUT0 + HALF]
+        for k in range(3):
+            for j in range(0, 8, 2):
+                c = 128 * (k // 2)
+                even, odd = wq[h, j, :, c : c + 128], wq[h, j + 1, :, c : c + 128]
+                sh = 64 * (k % 2)
+                at = k * D + h * HALF + 64 * j
+                o_qkv[:, at : at + 128] = jnp.where(lane < 64, roll(even, -sh), roll(odd, 64 - sh))
+    for k in range(32):
+        c = GFC0 + 128 * (k // 2)
+        o_fc[:, 128 * k : 128 * k + 128] = quarters(
+            [
+                roll(w4[a % 2, :, c : c + 128], 32 * a - 32 * ((2 * k + a // 2) % 4))
+                for a in range(4)
+            ]
+        )
+
+
+def kernel(
+    w_qkv,
+    w_out,
+    w_fc,
+    gains,
+    shifts,
+    attn_biases,
+    branch_biases,
+    fc_bias,
+    tokens,
+    cot,
+    wproj,
+    o_block,
+    o_in,
+    o_w4,
+    o_wq,
+    o_wp,
+    o_small,
+    *scratch,
+):
     names = list(SCRATCH)
     r = dict(zip(names, scratch[: len(names)]))
+    wpack = r["pack"]
     stages = scratch[len(names) :]
     r["dkv"] = r["sbuf"].at[:, 0 : 2 * HEAD]
     r["dh1"] = r["outp"]
@@ -346,104 +463,140 @@
         y=lax.div(sq, 4),
         z=lax.rem(lax.div(sq, 2), 2) * 2 + lax.rem(dp, 2),
     )
+    my, mz = me["y"], lax.div(me["z"], 2)
     j_me = lax.div(sq, 2)
     partner = (dp, sq + 1 - 2 * core)
 
-    peers = [dev(shift(me, a, d), core) for a in "xyz" for d in (1, -1)]
-    peers.append(partner)
-    for dyy, dzz in ((0, 2), (2, 0), (1, 2), (2, 2), (3, 2)):
-        peers.append(dev(shift(shift(me, "y", dyy), "z", dzz), core))
+    def seq_peer(t):
+        jj = lax.rem(j_me + t, 8)
+        return jj, (dp, jj * 2 + core)
+
+    def dp_peer(t):
+        ii = lax.rem(dp + t, 8)
+        return ii, (ii, sq)
+
+    peers = [partner, dev(shift(me, "z", 2 * lax.rem(me["z"], 2) - 1), core)]
+    for t in range(1, 8):
+        peers += [seq_peer(t)[1], dp_peer(t)[1]]
     bar = pltpu.get_barrier_semaphore()
     for t in peers:
         pl.semaphore_signal(bar, inc=1, device_id=t, device_id_type=MESH)
+    vectors = (gains, shifts, attn_biases, branch_biases)
+    pack(wpack, r["tiny"], w_qkv, w_out, w_fc, vectors, fc_bias)
     pl.semaphore_wait(bar, len(peers))
 
+    def sems(name):
+        return r[name + "_s"], r[name + "_r"]
+
     def pair(src, dst, i):
-        return pltpu.make_async_remote_copy(
-            src_ref=src,
-            dst_ref=dst,
-            send_sem=r["px_s"].at[i],
-            recv_sem=r["px_r"].at[i],
-            device_id=partner,
-            device_id_type=MESH,
-        )
+        return remote_copy(src, dst, sems("px"), i, partner)
 
     mine_rows = pl.ds(pl.multiple_of(core * 128, 128), 128)
     their_rows = pl.ds(pl.multiple_of(128 - core * 128, 128), 128)
     half0 = pl.multiple_of(core * HALF, HALF)
     half1 = pl.multiple_of(HALF - core * HALF, HALF)
-    own = (me["x"], lax.rem(me["z"], 2), me["y"], lax.div(me["z"], 2))
-
-    def partner_dev_j(t):
-        jj = lax.rem(j_me + t, 8)
-        return jj, (dp, jj * 2 + core)
-
-    def a2a(k, t, src, dst, to):
-        return pltpu.make_async_remote_copy(
-            src_ref=src,
-            dst_ref=dst,
-            send_sem=r["a2a_s"].at[k * 8 + t],
-            recv_sem=r["a2a_r"].at[k * 8 + t],
-            device_id=to,
-            device_id_type=MESH,
-        )
+    own = (me["x"], lax.rem(me["z"], 2), me["y"], mz)
 
     def tok(jj):
         return pl.ds(pl.multiple_of(jj * T, T), T)
 
+    class Swap:
+        def __init__(self, name, k, peer, at, send, land):
+            self.name, self.k, self.peer, self.at = name, k, peer, at
+            self.send, self.land = send, land
+
+        def copy(self, t):
+            pp, to = self.peer(t)
+            return remote_copy(
+                self.send(pp), self.land(self.at), sems(self.name), self.k * 8 + t, to
+            )
+
+        def start(self):
+            for t in range(1, 8):
+                self.copy(t).start()
+
+        def wait(self):
+            for t in range(1, 8):
+                pp = lax.rem(self.at + 8 - t, 8)
+                remote_copy(
+                    self.send(pp), self.land(pp), sems(self.name), self.k * 8 + t, partner
+                ).wait_recv()
+
+        def drain(self):
+            for t in range(1, 8):
+                self.copy(t).wait_send()
+
+    def seq_swap(k, send, land):
+        return Swap("a2a", k, seq_peer, j_me, send, land)
+
+    def dp_swap(k, send, land):
+        return Swap("dp", k, dp_peer, dp, send, land)
+
     px_w = pair(wpack.at[1 - core], r["wrecv"], 0)
     px_w.start()
-    px_x = pair(tokens, r["x"].at[mine_rows], 1)
-    px_x.start()
-    px_dy = pair(cot, r["dy"].at[mine_rows], 2)
-    px_dy.start()
+
     lc = [
-        pltpu.make_async_copy(tokens, r["x"].at[mine_rows], r["loc"].at[0]),
-        pltpu.make_async_copy(cot, r["dy"].at[mine_rows], r["loc"].at[1]),
-        pltpu.make_async_copy(wproj, r["wp"].at[own], r["loc"].at[2]),
+        pltpu.make_async_copy(tokens, r["x"].at[mine_rows], r["loc"].at[1]),
+        pltpu.make_async_copy(cot, r["dy"].at[mine_rows], r["loc"].at[2]),
+        pltpu.make_async_copy(wproj, r["wp"].at[own], r["loc"].at[3]),
     ]
     for c in lc:
         c.start()
+    px_x = pair(tokens, r["x"].at[mine_rows], 1)
+    px_dy = pair(cot, r["dy"].at[mine_rows], 2)
+
     px_w.wait_recv()
     mine, theirs = wpack[core], r["wrecv"][...]
     first = jnp.where(core == 0, mine, theirs)
     second = jnp.where(core == 0, theirs, mine)
     r["w4"][own] = jnp.concatenate([first, second], axis=0).astype(BF16)
-    lc[2].wait()
+    for c in lc:
+        c.wait()
 
     def gathers(table, base):
         out = []
         for i, (name, c0, n, rot) in enumerate(table):
-            out.append(Gather(me, core, r[name], c0, n, rot, r["ag_s"], r["ag_r"], (base + i) * 12))
+            out.append(Gather(me, core, r[name], c0, n, rot, sems("ag"), (base + i) * 12))
         return out
 
     ga = gathers(GATHER_A, 0)
-    gb = gathers(GATHER_B, len(GATHER_A))
-    for ph in range(2):
-        for g in ga + gb:
-            g.start(ph)
-        for g in ga + gb:
-            g.forward(ph)
-        for g in ga + gb:
-            g.finish(ph)
+    gb = gathers(GATHER_B, 3)
+    gc = gathers(GATHER_C, 6)
+    for g in ga + gb + gc:
+        g.start(0)
+    px_x.start()
+    px_dy.start()
+    for g in ga + gb + gc:
+        g.forward(0)
     for g in ga:
+        g.finish(0)
+        g.start(1)
+    for g in gb + gc:
+        g.finish(0)
+        g.start(1)
+    for g in ga:
+        g.forward(1)
+    for g in ga:
+        g.finish(1)
         g.start(2)
+    for g in gb + gc:
+        g.forward(1)
     for g in ga:
         g.forward(2)
-    for g in gb:
-        g.start(2)
-    lc[0].wait()
-    lc[1].wait()
     px_x.wait_recv()
     for g in ga:
         g.finish(2)
+    for g in gb:
+        g.finish(1)
+        g.start(2)
 
     lane = lax.broadcasted_iota(jnp.int32, (8, 128), 1)
     vec_t = [jnp.zeros((8, 128), F32) for _ in range(8)]
     fcb_t = [jnp.zeros((8, 128), F32) for _ in range(16)]
     for p in range(64):
-        tile = r["w4"][p // 16, (p // 8) % 2, (p // 2) % 4, p % 2, :, SMALL0 : SMALL0 + 128]
-        tile = tile.astype(F32)
+        tile = r["w4"][
+            p // 16, (p // 8) % 2, (p // 2) % 4, p % 2, :, SMALL0 : SMALL0 + 128
+        ].astype(F32)
         lo, hi = tile[0:8], tile[8:16]
         at = 16 * (p % 8)
         both = jnp.where(lane < 8, lo, 0.0) + pltpu.roll(jnp.where(lane < 8, hi, 0.0), 8, 1)
@@ -474,20 +627,40 @@
         if k == 2:
             v = v + r["vec"][5:6, pl.ds(half0, HALF)]
         r["qkvs"][k] = v.T.astype(BF16).reshape(8, HEAD, T)
-
-    def send_a2a1(start):
-        for t in range(1, 8):
-            jj, to = partner_dev_j(t)
-            c = a2a(0, t, r["qkvs"].at[:, jj], r["qkvt"].at[:, :, tok(j_me)], to)
-            c.start() if start else c.wait_send()
-
-    send_a2a1(True)
+    qkv_swap = seq_swap(0, lambda j: r["qkvs"].at[:, j], lambda j: r["qkvt"].at[:, :, tok(j)])
+    qkv_swap.start()
     r["qkvt"][:, :, tok(j_me)] = r["qkvs"][:, j_me]
+    for g in gc:
+        g.finish(1)
     for g in gb:
         g.forward(2)
-    for t in range(1, 8):
-        jj = lax.rem(j_me + 8 - t, 8)
-        a2a(0, t, r["qkvs"].at[:, jj], r["qkvt"].at[:, :, tok(jj)], partner).wait_recv()
+    for g in gc:
+        g.start(2)
+
+    def hcopy(src, dst, i, axis, d):
+        return remote_copy(src, dst, sems("xg"), i, dev(shift(me, axis, d), core))
+
+    def hrows(yy, zz, row, n):
+        return r["hs"].at[yy, zz, core, pl.ds(row, n)]
+
+    def h_from(yy, zz, row, n, i):
+        ref = hrows(yy, zz, row, n)
+        hcopy(ref, ref, i, "y", 1).wait_recv()
+
+    every = slice(None)
+    ym, yp, opposite = mod4(my - 1), mod4(my + 1), mod4(my + 2)
+    h_z = hcopy(hrows(my, mz, 0, 128), hrows(my, mz, 0, 128), 0, "z", 2)
+    h_y = [
+        hcopy(hrows(my, every, 0, 128), hrows(my, every, 0, 128), 1 + way(d), "y", d)
+        for d in (1, -1)
+    ]
+    h_f = [
+        hcopy(hrows(ym, every, 0, 64), hrows(ym, every, 0, 64), 3, "y", 1),
+        hcopy(hrows(yp, every, 64, 64), hrows(yp, every, 64, 64), 4, "y", -1),
+    ]
+    h1s = r["hs"].reshape(LEN, D)
+    k_t, v_t = r["qkvt"].at[1], r["qkvt"].at[2]
+    qkv_swap.wait()
 
     r["qz"][0:HEAD, :] = r["qkvt"][0]
     r["qz"][HEAD:, :] = jnp.zeros((HEAD, LEN), BF16)
@@ -501,7 +674,7 @@
 
         lax.fori_loop(0, LEN // JB, one, 0)
 
-    to_rows(r["kv"], [lambda cols: r["qkvt"][1, :, cols], lambda cols: r["qkvt"][2, :, cols]])
+    to_rows(r["kv"], [lambda cols: k_t[:, cols], lambda cols: v_t[:, cols]])
 
     row_i = lax.broadcasted_iota(jnp.int32, (JB, IB), 0)
     col_i = lax.broadcasted_iota(jnp.int32, (JB, IB), 1)
@@ -532,7 +705,7 @@
             l, o = state
             p = jnp.exp2(r["sbuf"][jcols(jb), :] * SCALE2 - m)
             l = l + fold8(p)
-            return l, o + nn(r["qkvt"][2, :, jcols(jb)], p.astype(BF16))
+            return l, o + nn(v_t[:, jcols(jb)], p.astype(BF16))
 
         l, o = lax.fori_loop(
             0, nfull + 1, weigh, (jnp.zeros((8, IB), F32), jnp.zeros((HEAD, IB), F32))
@@ -542,19 +715,18 @@
         r["ot"][:, icols] = o
         r["ots"][:, icols] = o.astype(BF16)
         r["lse"][:, icols] = jnp.broadcast_to(m + jnp.log2(l), (8, IB))
+
+        @pl.when(ib == 5)
+        def _():
+            for g in gc:
+                g.forward(2)
+
         return c
 
     lax.fori_loop(0, LEN // IB, attend, 0)
-
-    def send_a2a2(start):
-        for t in range(1, 8):
-            jj, to = partner_dev_j(t)
-            c = a2a(1, t, r["ots"].at[:, tok(jj)], r["attt"].at[j_me], to)
-            c.start() if start else c.wait_send()
-
-    send_a2a2(True)
+    att_swap = seq_swap(1, lambda j: r["ots"].at[:, tok(j)], lambda j: r["attt"].at[j])
+    att_swap.start()
     r["attt"][j_me] = r["ots"][:, tok(j_me)]
-
     for g in gb:
         g.finish(2)
     keep = r["w4"].at[pl.ds(2 * core, 2), :, :, :, :, pl.ds(OUT0, HALF)]
@@ -562,11 +734,13 @@
     wor_mine = r["wor"].at[:, :, :, :, :, pl.ds(half0, HALF)]
     px_wo = pair(give, wor_mine, 3)
     px_wo.start()
-    lc_wo = pltpu.make_async_copy(keep, wor_mine, r["loc"].at[3])
+    lc_wo = pltpu.make_async_copy(keep, wor_mine, r["loc"].at[4])
     lc_wo.start()
-    for t in range(1, 8):
-        jj = lax.rem(j_me + 8 - t, 8)
-        a2a(1, t, r["ots"].at[:, tok(jj)], r["attt"].at[jj], partner).wait_recv()
+    lc_h = pltpu.make_async_copy(r["h1"].at[mine_rows], r["hs"].at[my, mz, core], r["loc"].at[5])
+    lc_h.start()
+    lc_h.wait()
+    h_z.start()
+    att_swap.wait()
     lc_wo.wait()
     px_wo.wait_recv()
 
@@ -585,9 +759,12 @@
 
     rows_loop(T, 32, ln2)
     r["h2t"][...] = r["h2"][...].astype(F32).T.astype(BF16)
-    r["outp"][...] = jnp.zeros((T, D), F32)
-    r["dh"][...] = jnp.zeros((T, D), F32)
     px_dy.wait_recv()
+    h_from(my, 1 - mz, 0, 128, 0)
+    for c in h_y:
+        c.start()
+    for g in gc:
+        g.finish(2)
 
     def ffn(t, c):
         hi, lo = lax.div(t, 2), lax.rem(t, 2)
@@ -603,37 +780,46 @@
             0.7978845608028654 * (1.0 + 3.0 * 0.044715 * sq_)
         )
         d_pre = (slope * d_act).astype(BF16)
-        r["outp"][...] += nn(act.astype(BF16), wp)
-        r["gp"][hi, lo] = (
-            nn(act.T.astype(BF16), r["dy"][...]).astype(BF16).reshape(4, 2, 32, D)
-        )
-        r["g4"][:, :, :, :, :, pl.ds(pl.multiple_of(GFC0 + t * 256, 256), 256)] = (
-            nn(r["h2t"][...], d_pre).astype(BF16).reshape(4, 2, 4, 2, 16, 256)
-        )
+        r["act"][:, cols] = act.astype(BF16)
+        r["dpre"][:, cols] = d_pre
         r["sfc"][:, cols] = jnp.broadcast_to(
             jnp.sum(d_pre.astype(F32), axis=0, keepdims=True), (8, 256)
         )
-        r["dh"][...] += nt(d_pre, wf)
+
         return c
 
     lax.fori_loop(0, 8, ffn, 0)
 
+    def ffn_dh(n, c):
+        cols = pl.ds(pl.multiple_of(n * 256, 256), 256)
+        r["dh"][:, cols] = nt(r["dpre"][...], r["w4"][n, :, :, :, :, FC0:].reshape(256, FFH))
+        return c
+
+    lax.fori_loop(0, 4, ffn_dh, 0)
     px_dh = pair(r["dh"], r["dhr"], 5)
     px_dh.start()
-    px_out = pair(r["outp"].at[their_rows], r["outr"], 6)
-    px_out.start()
 
     def reduces(table, base, stage_at):
         out = []
         for i, (name, c0, n, rot) in enumerate(table):
-            piece = Reduce(me, core, r[name], c0, n, rot, r["rs_s"], r["rs_r"], (base + i) * 12)
+            piece = Reduce(me, core, r[name], c0, n, rot, sems("rs"), (base + i) * 12)
             k = (stage_at + i) * 9
             out.append(piece.attach(stages[k : k + 9]))
         return out
 
-    rf = reduces(REDUCE_F, 0, 0)
-    rq = reduces(REDUCE_Q, len(REDUCE_F), len(REDUCE_F))
-    for g in rf:
+    rp = reduces(REDUCE_P, 0, 0)
+    rf = reduces(REDUCE_F, 2, 2)
+    ro = reduces(REDUCE_O, 6, 6)
+
+    def grad_proj(t, c):
+        hi, lo = lax.div(t, 2), lax.rem(t, 2)
+        cols = pl.ds(pl.multiple_of(t * 256, 256), 256)
+        act_t = r["act"][:, cols].astype(F32).T.astype(BF16)
+        r["gp"][hi, lo] = nn(act_t, r["dy"][...]).astype(BF16).reshape(4, 2, 32, D)
+        return c
+
+    lax.fori_loop(0, 8, grad_proj, 0)
+    for g in rp:
         g.start(0)
 
     r["sv"][...] = jnp.zeros((8, D), F32)
@@ -653,15 +839,34 @@
     wor = r["wor"][...].reshape(HALF, D)
     r["datt"][...] = nt(wor, r["dbr"][...]).astype(BF16).reshape(8, HEAD, T)
 
-    def send_a2a3(start):
-        for t in range(1, 8):
-            jj, to = partner_dev_j(t)
-            c = a2a(2, t, r["datt"].at[jj], r["dz"].at[pl.ds(HEAD, HEAD), tok(j_me)], to)
-            c.start() if start else c.wait_send()
-
-    send_a2a3(True)
+    datt_swap = seq_swap(
+        2, lambda j: r["datt"].at[j], lambda j: r["dz"].at[pl.ds(HEAD, HEAD), tok(j)]
+    )
+    datt_swap.start()
     r["dz"][HEAD:, tok(j_me)] = r["datt"][j_me]
     r["dz"][0:HEAD, :] = jnp.zeros((HEAD, LEN), BF16)
+
+    def grad_fc(t, c):
+        cols = pl.ds(pl.multiple_of(GFC0 + t * 256, 256), 256)
+        r["g4"][:, :, :, :, :, cols] = (
+            nn(r["h2t"][...], r["dpre"][:, pl.ds(pl.multiple_of(t * 256, 256), 256)])
+            .astype(BF16)
+            .reshape(4, 2, 4, 2, 16, 256)
+        )
+        return c
+
+    lax.fori_loop(0, 8, grad_fc, 0)
+    for g in rf:
+        g.start(0)
+
+    def ffn_out(n, c):
+        cols = pl.ds(pl.multiple_of(n * 256, 256), 256)
+        r["outp"][:, cols] = nn(r["act"][...], r["wp"][:, :, :, :, :, cols].reshape(FFH, 256))
+        return c
+
+    lax.fori_loop(0, 4, ffn_out, 0)
+    px_out = pair(r["outp"].at[their_rows], r["outr"], 6)
+    px_out.start()
 
     gout = nn(r["attt"][...].reshape(HALF, T), r["dbr"][...]).astype(BF16)
     left = gout[:, :HALF].reshape(2, 2, 4, 2, 16, HALF)
@@ -702,12 +907,16 @@
     lax.fori_loop(0, 4, block_out, 0)
     px_out.wait_send()
 
-    for g in rf:
+    h_from(ym, every, 0, 128, 1)
+    h_f[0].start()
+    h_from(yp, every, 0, 128, 2)
+    h_f[1].start()
+    px_go.wait_recv()
+    for g in ro:
+        g.start(0)
+    for g in rp:
         g.forward(0)
-
-    for t in range(1, 8):
-        jj = lax.rem(j_me + 8 - t, 8)
-        a2a(2, t, r["datt"].at[jj], r["dz"].at[pl.ds(HEAD, HEAD), tok(jj)], partner).wait_recv()
+    datt_swap.wait()
 
     to_rows(r["qd"], [lambda cols: r["qz"][0:HEAD, cols], lambda cols: r["dz"][HEAD:, cols]])
     r["rowdot"][...] = jnp.broadcast_to(
@@ -715,6 +924,8 @@
     )
     r["dkv"][...] = jnp.zeros((LEN, 2 * HEAD), F32)
     lane_kv = lax.broadcasted_iota(jnp.int32, (JB, 2 * HEAD), 1)
+
+    px_h = pair(r["hs"].at[:, :, core], r["hs"].at[:, :, core], 12)
 
     def attend_back(ib, c):
         icols = pl.ds(pl.multiple_of(ib * IB, IB), IB)
@@ -732,24 +943,27 @@
             r["dkv"][jcols(jb), :] += jnp.where(
                 lane_kv < HEAD, nn(ds, qd), nn(p.astype(BF16), qd)
             )
-            return dq + nn(r["qkvt"][1, :, jcols(jb)], ds)
+            return dq + nn(k_t[:, jcols(jb)], ds)
 
         dq = lax.fori_loop(
             0, nfull, lambda jb, a: step(jb, a, False), jnp.zeros((HEAD, IB), F32)
         )
         r["dqt"][:, icols] = step(nfull, dq, True)
 
-        @pl.when(ib == 3)
+        @pl.when(ib == 2)
         def _():
-            for g in rf:
-                g.finish(0)
-            for g in rf:
-                g.start(1)
+            rf[0].forward(0)
+
+        @pl.when(ib == 6)
+        def _():
+            h_from(opposite, every, 0, 64, 3)
+            h_from(opposite, every, 64, 64, 4)
+            px_h.start()
 
         @pl.when(ib == 5)
         def _():
-            for g in rf:
-                g.forward(1)
+            for g in rf[1:] + ro:
+                g.forward(0)
 
         return c
 
@@ -765,31 +979,29 @@
 
     lax.fori_loop(0, LEN // JB, kv_back, 0)
 
-    def send_a2a4(start):
-        for t in range(1, 8):
-            jj, to = partner_dev_j(t)
-            c = a2a(3, t, r["dqkvt"].at[:, :, tok(jj)], r["dqs"].at[:, j_me], to)
-            c.start() if start else c.wait_send()
-
-    send_a2a4(True)
+    dqkv_swap = seq_swap(3, lambda j: r["dqkvt"].at[:, :, tok(j)], lambda j: r["dqs"].at[:, j])
+    dqkv_swap.start()
     r["dqs"][:, j_me] = r["dqkvt"][:, :, tok(j_me)]
-    for g in rf:
-        g.finish(1)
-    for g in rf:
-        g.start(2)
-    for t in range(1, 8):
-        jj = lax.rem(j_me + 8 - t, 8)
-        a2a(3, t, r["dqkvt"].at[:, :, tok(jj)], r["dqs"].at[:, jj], partner).wait_recv()
-
-    h1t = r["h1"][...].astype(F32).T.astype(BF16)
-    for k in range(3):
-        dt = r["dqs"][k].reshape(HALF, T)
-        r["g4"][:, :, :, :, :, k * HALF : (k + 1) * HALF] = (
-            nt(h1t, dt).astype(BF16).reshape(4, 2, 4, 2, 16, HALF)
-        )
-    px_go.wait_recv()
-    for g in rq[:3]:
-        g.start(0)
+
+    px_h.wait_recv()
+    d192 = r["dqkvt"][...].reshape(3 * HEAD, LEN)
+    for k in range(4):
+        g = nn(d192, h1s[:, 256 * k : 256 * k + 256]).astype(BF16)
+        r["gqs"][2 * k] = g[:, :128]
+        r["gqs"][2 * k + 1] = g[:, 128:]
+    gq_swap = dp_swap(1, lambda i: r["gqs"].at[i], lambda i: r["gqr"].at[i])
+    gq_swap.start()
+    r["gqr"][dp] = r["gqs"][dp]
+    for g in rp:
+        g.finish(0)
+        g.start(1)
+    for g in rf[:1]:
+        g.finish(0)
+        g.start(1)
+    for g in rp:
+        g.forward(1)
+    dqkv_swap.wait()
+
     for k in range(3):
         d = r["dqs"][k].reshape(HALF, T).astype(F32).T
         if k != 1:
@@ -800,7 +1012,29 @@
         r["dh1"][...] = v if k == 0 else r["dh1"][...] + v
     px_d1 = pair(r["dh1"].at[their_rows], r["dh1r"], 8)
     px_d1.start()
-    for g in rf:
+    for g in rf[:1]:
+        g.forward(1)
+    for g in rf[1:] + ro:
+        g.finish(0)
+        g.start(1)
+    for g in rp:
+        g.finish(1)
+        g.start(2)
+    gq_swap.wait()
+    total = r["gqr"][0].astype(F32)
+    for i in range(1, 8):
+        total = total + r["gqr"][i].astype(F32)
+    total = jnp.concatenate([total, jnp.zeros((HEAD, 128), F32)], axis=0)
+    r["gqt"][...] = total.T.reshape(8, 16, 256)
+    gqt_swap = seq_swap(4, lambda j: r["gqt"].at[j], lambda j: r["finq"].at[j])
+    gqt_swap.start()
+    r["finq"][j_me] = r["gqt"][j_me]
+    for g in rf[:1]:
+        g.finish(1)
+        g.start(2)
+    for g in rf[1:] + ro:
+        g.forward(1)
+    for g in rp:
         g.forward(2)
     px_d1.wait_recv()
 
@@ -818,66 +1052,68 @@
     for row, s in zip((0, 2), sums):
         r["sv"][row : row + 1, :] = jnp.sum(s, axis=0, keepdims=True)
 
-    for p in range(64):
-        k, at = p // 8, 16 * (p % 8)
-        v = r["sv"][:, 128 * k : 128 * k + 128]
-        v = pltpu.roll(v, (128 - at) % 128, 1) if at else v
-        k, sh = p // 4, (32 - 32 * (p % 4)) % 128
-        f = r["sfc"][:, 128 * k : 128 * k + 128]
-        f = pltpu.roll(f, sh, 1) if sh else f
-        r["gs"][p // 16, (p // 8) % 2, (p // 2) % 4, p % 2] = jnp.where(
-            lane < 16, v, jnp.where((lane >= 32) & (lane < 64), f, 0.0)
-        )
-    rq[3].start(0)
-
-    def out_of(g, wide, tall):
-        return wide.at[:, pl.ds(g.c0, g.n)] if tall is None else tall.at[:, pl.ds(g.c0, g.n)]
-
-    for ph in range(3):
-        for g in rq:
-            g.forward(ph)
-        if ph == 0:
-            for g in rf:
-                g.finish(2, out_of(g, r["fin"], o_wp if g.ref is r["gp"] else None))
-        for i, g in enumerate(rq):
-            out = None
-            if ph == 2:
-                out = r["fins"] if i == 3 else out_of(g, r["fin"], None)
-            g.finish(ph, out)
-            if ph < 2:
-                g.start(ph + 1)
+    for i in range(8):
+        r["ss"][i, 0:8] = r["sv"][:, 128 * i : 128 * i + 128]
+        r["ss"][i, 8:9] = r["sfc"][0:1, 256 * i : 256 * i + 128]
+        r["ss"][i, 9:10] = r["sfc"][0:1, 256 * i + 128 : 256 * i + 256]
+        r["ss"][i, 10:16] = jnp.zeros((6, 128), F32)
+    ss_swap = dp_swap(2, lambda i: r["ss"].at[i], lambda i: r["ssr"].at[i])
+    ss_swap.start()
+    r["ssr"][dp] = r["ss"][dp]
+    for g in rf[1:] + ro:
+        g.finish(1)
+        g.start(2)
+    for g in rf[:1]:
+        g.forward(2)
+    ss_swap.wait()
+    r["st"][...] = jnp.sum(r["ssr"][...], axis=0)
+    st_swap = seq_swap(5, lambda j: r["st"], lambda j: r["str"].at[j])
+    st_swap.start()
+    r["str"][j_me] = r["st"][...]
 
     mine8 = pl.ds(pl.multiple_of(core * 8, 8), 8)
     their8 = pl.ds(pl.multiple_of(8 - core * 8, 8), 8)
+    for g in rf[1:] + ro:
+        g.forward(2)
+    gqt_swap.wait()
+    px_q = pair(r["finq"].at[:, their8], o_wq.at[core], 11)
+    px_q.start()
+    o_wq[core] = r["finq"][:, mine8, :]
+    for g in rp + rf + ro:
+        tall = g.ref is r["gp"]
+        g.finish(2, (o_wp if tall else r["fin"]).at[:, pl.ds(g.c0, g.n)])
     px_f = pair(r["fin"].at[their8], o_w4.at[core], 9)
     px_f.start()
+    o_w4[core] = r["fin"][mine8, :]
+    st_swap.wait()
+    r["fins"][...] = jnp.sum(r["str"][...], axis=0)
     px_s = pair(r["fins"], r["finr"], 10)
     px_s.start()
-    o_w4[core] = r["fin"][mine8, :]
+    px_s.wait_recv()
+    total = r["fins"][0:8, :] + r["finr"][0:8, :]
+    total = pltpu.roll(total, lax.rem(128 - (16 * j_me + 8 * core), 128), 1)
+    fc = jnp.where(lax.div(j_me, 4) == 0, r["fins"][8:9, :], r["fins"][9:10, :])
+    fc = pltpu.roll(jnp.broadcast_to(fc, (8, 128)), lax.rem(160 - 32 * lax.rem(j_me, 4), 128), 1)
+    o_small[...] = jnp.where(lane < 8, total, fc)
+    px_q.wait_recv()
     px_f.wait_recv()
-    px_s.wait_recv()
-    total = r["fins"][...] + jnp.where(lane < 16, r["finr"][...], 0.0)
-    shifted = jnp.where(core == 0, total, pltpu.roll(total, 120, 1))
-    o_small[...] = jnp.where(lane < 8, shifted, total)
-
-    for g in ga + gb + rf + rq:
+
+    for g in ga + gb + gc + rp + rf + ro:
         g.drain()
-    for c in (px_w, px_x, px_dy, px_wo, px_dh, px_go, px_d1, px_f, px_s):
+    for g in (qkv_swap, att_swap, datt_swap, dqkv_swap, gq_swap, gqt_swap, ss_swap, st_swap):
+        g.drain()
+    for c in (px_w, px_x, px_dy, px_wo, px_dh, px_go, px_d1, px_q, px_f, px_s, px_h, h_z, *h_y, *h_f):
         c.wait_send()
-    send_a2a1(False)
-    send_a2a2(False)
-    send_a2a3(False)
-    send_a2a4(False)
 
 
 def stage_list():
     out = []
-    for name, _, n, rot in REDUCE_F + REDUCE_Q:
-        out += Reduce.stage_shapes(ROWS[name], n, rot, TYPES[name])
+    for name, _, n, rot in REDUCE_P + REDUCE_F + REDUCE_O:
+        out += Reduce.stage_shapes(ROWS[name], n, rot, BF16)
     return out
 
 
-def block(wpack, tokens, cot, wproj):
+def block(*args):
     vm = pl.BlockSpec(memory_space=pltpu.VMEM)
     return pl.pallas_call(
         kernel,
@@ -885,16 +1121,40 @@
             jax.ShapeDtypeStruct((128, D), BF16),
             jax.ShapeDtypeStruct((128, D), BF16),
             jax.ShapeDtypeStruct((2, 8, G4), F32),
+            jax.ShapeDtypeStruct((2, 8, 8, 256), F32),
             jax.ShapeDtypeStruct((32, D), F32),
             jax.ShapeDtypeStruct((8, 128), F32),
         ),
-        in_specs=[vm] * 4,
-        out_specs=(vm,) * 5,
+        in_specs=[vm] * len(args),
+        out_specs=(vm,) * 6,
         scratch_shapes=list(SCRATCH.values()) + stage_list(),
         compiler_params=pltpu.CompilerParams(
             collective_id=0, has_side_effects=True, vmem_limit_bytes=63 * 2**20
         ),
-    )(wpack, tokens, cot, wproj)
+    )(*args)
+
+
+def outputs(*results):
+    vm = pl.BlockSpec(memory_space=pltpu.VMEM)
+    vector = jax.ShapeDtypeStruct((2, 8), F32)
+    return pl.pallas_call(
+        unpack,
+        out_shape=(
+            jax.ShapeDtypeStruct((128, D), BF16),
+            jax.ShapeDtypeStruct((128, D), BF16),
+            vector,
+            vector,
+            jax.ShapeDtypeStruct((8, 3 * D), F32),
+            vector,
+            jax.ShapeDtypeStruct((8, D), F32),
+            vector,
+            jax.ShapeDtypeStruct((8, FF), F32),
+            jax.ShapeDtypeStruct((1, 32), F32),
+            jax.ShapeDtypeStruct((32, D), F32),
+        ),
+        in_specs=[vm] * len(results),
+        out_specs=(vm,) * 11,
+    )(*results)
 
 
 def on_device(
@@ -910,32 +1170,32 @@
     w_proj,
     cotangent,
 ):
-    q = w_qkv.reshape(8, 3, 2, HALF).transpose(2, 0, 1, 3).reshape(2, 8, 3 * HALF)
-    o = w_out.reshape(8, 2, HALF).transpose(1, 0, 2)
-    f = w_fc.reshape(8, 64, 2, 32).transpose(2, 0, 1, 3).reshape(2, 8, FFH)
-    vectors = jnp.concatenate([norm_gains, norm_biases, attn_biases, branch_biases], axis=0)
-    fcb = jnp.concatenate([fc_bias[None], jnp.zeros((7, 32), BF16)], axis=0)
-    small = jnp.concatenate(
-        [vectors, jnp.zeros((8, 24), BF16), fcb, jnp.zeros((8, 64), BF16)], axis=1
+    results = block(
+        w_qkv,
+        w_out,
+        w_fc,
+        norm_gains,
+        norm_biases,
+        attn_biases,
+        branch_biases,
+        fc_bias[None],
+        tokens[0],
+        cotangent[0],
+        w_proj,
     )
-    small = jnp.broadcast_to(small[None], (2, 8, 128))
-    wpack = jnp.concatenate([q, small, o, f], axis=2).astype(F32)
-    block_out, input_grad, gw4, gwp, gsmall = block(wpack, tokens[0], cotangent[0], w_proj)
-    gq = gw4[:, :, :GOUT0].reshape(2, 8, 3, HALF).transpose(1, 2, 0, 3).reshape(8, 3 * D)
-    go = gw4[:, :, GOUT0:GFC0].transpose(1, 0, 2).reshape(8, D)
-    gf = gw4[:, :, GFC0:].reshape(2, 8, 64, 32).transpose(1, 2, 0, 3).reshape(8, FF)
+    block_out, input_grad, gains, shifts, qkv, attn, out, branch, fc, fcb, proj = outputs(*results)
     return (
         block_out[None],
         input_grad[None],
-        gsmall[0:2, :8],
-        gsmall[2:4, :8],
-        gq,
-        gsmall[4:6, :8],
-        go,
-        gsmall[6:8, :8],
-        gf,
-        gsmall[0, 32:64],
-        gwp,
+        gains,
+        shifts,
+        qkv,
+        attn,
+        out,
+        branch,
+        fc,
+        fcb[0],
+        proj,
     )
 
 

time: 207 us -> 172 us (0.83)
  Pallas kernels: 192 us -> 172 us
  local copies, waits for them, and re-layouts: 12.1 us -> 0 us
    pallas_call x1, Pallas kernels: 192 us -> 169 us  [block(): pl.pallas_call(kernel, out_shape=(jax.ShapeDtypeStruct((128, D), BF16), j...]
    slice x4 -> x0, local copies, waits for them, and re-layouts: 3.68 us -> none  [the longest x1 1.4 us: on_device(): gsmall[6:8, :8]]
    unnamed x15 -> x0, local copies, waits for them, and re-layouts: 3.14 us -> none
    reshape x5 -> x0, local copies, waits for them, and re-layouts: 2.75 us -> none  [the longest x2 1.49 us: on_device(): gw4[:, :, GFC0:].reshape(2, 8, 64, 32).transpose(1, 2, 0, 3).reshape(8, FF)]
    pallas_call x0 -> x1, Pallas kernels: none -> 2.29 us  [outputs(): pl.pallas_call(unpack, out_shape=(jax.ShapeDtypeStruct((128, D), BF16), j...]
where the time goes in v2:
time: 172 us
  Pallas kernels  172 us (100%)
    pallas_call x1, Pallas kernels, block(): pl.pallas_call(kernel, out_shape=(jax.ShapeDtypeStruct((128, D), BF16), j...  169 us

profile of v2, /device:TPU:1, one launch (start us, length us, event | category | flops | bytes accessed | tf_op | source)
XLA Modules:
  0.0 172.3 jit_solution(9672924693983143445)
XLA Ops:
  0.6 169.3 %shard_map.194 = (bf16[128,1024]{1,0:T(8,128)(2,1)}, bf16[128,1024]{1,0:T(8,128)(2,1)}, f32[2,8,2560]{2,1,0:T(8,128)}, f32[2,8,8,256]{3,2,1,0:T(8,128)}, f32[32,1024]{1,0:T(8,128)}, /*index=5*/f32[8,128]{1,0:T(8,128)}) custom-call(bf16[8,3072]{1,0:T(8,128)(2,1)} %w_qkv.1, bf16[8,1024]{1,0:T(8,128)(2,1)} %w_out.1, bf16[8,4096]{1,0:T(8,128)(2,1)} %w_fc.1, ...), custom_call_target="tpu_custom_call" | custom-call | tf_op jit(solution)/shard_map/pallas_call | solution.py:1118
  170.0 2.3 %shard_map.195 = (bf16[128,1024]{1,0:T(8,128)(2,1)}, bf16[128,1024]{1,0:T(8,128)(2,1)}, f32[2,8]{1,0:T(2,128)}, f32[2,8]{1,0:T(2,128)}, f32[8,3072]{1,0:T(8,128)...) custom-call(bf16[128,1024]{1,0:T(8,128)(2,1)} %get-tuple-element.28., ...), custom_call_target="tpu_custom_call" | custom-call | tf_op jit(solution)/shard_map/pallas_call | solution.py:1140

commit v3 on v2

--- a/solution.py
+++ b/solution.py
@@ -135,6 +135,8 @@
             sel[a] = None if k < ph else (mod4(self.me[a] + off) if k == ph else self.me[a])
         return blocks(self.ref, sel, *self.cols(h))
 
+    direct = (0,)
+
     def ways1(self):
         return (1, -1) if self.n > 128 else (1,)
 
@@ -142,11 +144,19 @@
         r = self.region(ph, 0, None) if st == 0 else self.region(ph, -d, way(d))
         return self.remote(r, r, ph, st, d)
 
+    def across(self, ph, off):
+        r = self.region(ph, off, None)
+        return self.remote(r, r, ph, 1, 2)
+
     def start(self, ph):
         for d in (1, -1):
             self.copy(ph, 0, d).start()
+        if ph in self.direct:
+            self.across(ph, 0).start()
 
     def forward(self, ph):
+        if ph in self.direct:
+            return
         for d in (1, -1):
             r = self.region(ph, -d, None)
             self.remote(r, r, ph, 0, d).wait_recv()
@@ -154,6 +164,12 @@
                 self.copy(ph, 1, d).start()
 
     def finish(self, ph):
+        if ph in self.direct:
+            for d in (1, -1):
+                r = self.region(ph, -d, None)
+                self.remote(r, r, ph, 0, d).wait_recv()
+            self.across(ph, 2).wait_recv()
+            return
         for d in self.ways1():
             r = self.region(ph, -2 * d, way(d))
             self.remote(r, r, ph, 1, d).wait_recv()
@@ -162,8 +178,11 @@
         for ph in range(3):
             for d in (1, -1):
                 self.copy(ph, 0, d).wait_send()
-            for d in self.ways1():
-                self.copy(ph, 1, d).wait_send()
+            if ph in self.direct:
+                self.across(ph, 0).wait_send()
+            else:
+                for d in self.ways1():
+                    self.copy(ph, 1, d).wait_send()
 
 
 class Reduce(Piece):
@@ -173,14 +192,15 @@
 
     @staticmethod
     def stage_shapes(rows, n, rot, dtype):
-        out = []
         (_, n0), (_, n1) = half_split(n)
-        for ph in range(3):
-            lead = lead_dims(ORDERS[rot][: ph + 1])
-            out.append(pltpu.VMEM(lead + (rows, n0), dtype))
-            out.append(pltpu.VMEM(lead + (rows, max(n1, 128)), dtype))
-            out.append(pltpu.VMEM((2,) + lead + (rows, n), dtype))
-        return out
+        lead = [lead_dims(ORDERS[rot][: ph + 1]) for ph in range(3)]
+        return [
+            pltpu.VMEM(lead[0] + (rows, n0), dtype),
+            pltpu.VMEM(lead[0] + (rows, n1), dtype),
+            pltpu.VMEM((2,) + lead[0] + (rows, n), dtype),
+            pltpu.VMEM((3,) + lead[1] + (rows, n), dtype),
+            pltpu.VMEM((3,) + lead[2] + (rows, n), dtype),
+        ]
 
     def region(self, ph, off, h):
         sel = {}
@@ -188,24 +208,30 @@
             sel[a] = self.me[a] if k < ph else (mod4(self.me[a] + off) if k == ph else None)
         return blocks(self.ref, sel, *self.cols(h))
 
-    def ways0(self):
-        return (1, -1) if self.n > 128 else (1,)
-
     def copy(self, ph, st, d):
         if st == 0:
-            return self.remote(self.region(ph, 2, way(d)), self.stage[3 * ph + way(d)], ph, 0, d)
-        return self.remote(self.region(ph, d, None), self.stage[3 * ph + 2].at[way(d)], ph, 1, d)
+            return self.remote(self.region(ph, 2, way(d)), self.stage[way(d)], ph, 0, d)
+        return self.remote(self.region(ph, d, None), self.stage[2].at[way(d)], ph, 1, d)
+
+    def straight(self, ph, k):
+        d = (1, -1, 2)[k]
+        st = 1 if k == 2 else 0
+        return self.remote(self.region(ph, d, None), self.stage[2 + ph].at[k], ph, st, d)
 
     def start(self, ph):
-        for d in self.ways0():
-            self.copy(ph, 0, d).start()
-
-    def add(self, target, sources, lead):
+        if ph:
+            for k in range(3):
+                self.straight(ph, k).start()
+        else:
+            for d in (1, -1):
+                self.copy(0, 0, d).start()
+
+    def add(self, target, sources, lead, wide=False):
         def one(idx):
-            total = target[idx]
+            total = target[idx].astype(F32) if wide else target[idx]
             for s in sources:
-                total = total + s[idx]
-            target[idx] = total
+                total = total + s[idx].astype(total.dtype)
+            target[idx] = total.astype(target.dtype)
 
         if not lead:
             one(Ellipsis)
@@ -213,30 +239,40 @@
             lax.fori_loop(0, lead[0], lambda i, c: (one(i), c)[1], 0)
 
     def forward(self, ph):
-        lead = lead_dims(self.order[: ph + 1])
+        if ph:
+            return
+        lead = lead_dims(self.order[:1])
         for d in (1, -1):
-            if d in self.ways0():
-                self.copy(ph, 0, d).wait_recv()
-                self.add(self.region(ph, d, way(d)), [self.stage[3 * ph + way(d)]], lead)
-            self.copy(ph, 1, d).start()
+            self.copy(0, 0, d).wait_recv()
+            self.add(self.region(0, d, way(d)), [self.stage[way(d)]], lead)
+            self.copy(0, 1, d).start()
 
     def finish(self, ph, out=None):
         lead = lead_dims(self.order[: ph + 1])
-        s = self.stage[3 * ph + 2]
+        s = self.stage[2 + ph]
+        if ph:
+            for k in range(3):
+                self.straight(ph, k).wait_recv()
+        else:
+            for d in (1, -1):
+                self.copy(0, 1, d).wait_recv()
+        mine = self.region(ph, 0, None)
+        arrived = [s.at[k] for k in range(3 if ph else 2)]
+        if out is None:
+            self.add(mine, arrived, lead, wide=ph > 0)
+        else:
+            total = mine[...].astype(F32)
+            for a in arrived:
+                total = total + a[...].astype(F32)
+            out[...] = total
+
+    def drain(self):
         for d in (1, -1):
-            self.copy(ph, 1, d).wait_recv()
-        mine = self.region(ph, 0, None)
-        if out is None:
-            self.add(mine, [s.at[0], s.at[1]], lead)
-        else:
-            out[...] = mine[...].astype(F32) + s[0].astype(F32) + s[1].astype(F32)
-
-    def drain(self):
-        for ph in range(3):
-            for d in self.ways0():
-                self.copy(ph, 0, d).wait_send()
-            for d in (1, -1):
-                self.copy(ph, 1, d).wait_send()
+            self.copy(0, 0, d).wait_send()
+            self.copy(0, 1, d).wait_send()
+        for ph in (1, 2):
+            for k in range(3):
+                self.straight(ph, k).wait_send()
 
 
 GATHER_B = (
@@ -618,7 +654,7 @@
         r["h1"][rows, :] = (xhat * vrow(0) + vrow(2)).astype(BF16)
         return c
 
-    rows_loop(T, 32, ln1)
+    rows_loop(T, 128, ln1)
     for k in range(3):
         w = r["w4"][:, :, :, :, :, k * HALF : (k + 1) * HALF].reshape(D, HALF)
         v = nn(r["h1"][...], w)
@@ -757,7 +793,7 @@
         r["h2"][rows, :] = (xhat * vrow(1) + vrow(3)).astype(BF16)
         return c
 
-    rows_loop(T, 32, ln2)
+    rows_loop(T, 128, ln2)
     r["h2t"][...] = r["h2"][...].astype(F32).T.astype(BF16)
     px_dy.wait_recv()
     h_from(my, 1 - mz, 0, 128, 0)
@@ -767,10 +803,9 @@
         g.finish(2)
 
     def ffn(t, c):
-        hi, lo = lax.div(t, 2), lax.rem(t, 2)
-        cols = pl.ds(pl.multiple_of(t * 256, 256), 256)
-        wf = r["w4"][:, :, :, :, :, pl.ds(pl.multiple_of(FC0 + t * 256, 128), 256)].reshape(D, 256)
-        wp = r["wp"][hi, lo].reshape(256, D)
+        cols = pl.ds(pl.multiple_of(t * 512, 512), 512)
+        wf = r["w4"][:, :, :, :, :, pl.ds(pl.multiple_of(FC0 + t * 512, 128), 512)].reshape(D, 512)
+        wp = r["wp"][t].reshape(512, D)
         pre = nn(r["h2"][...], wf) + r["fcb"][0:1, cols]
         d_act = nt(r["dy"][...], wp)
         sq_ = pre * pre
@@ -783,12 +818,12 @@
         r["act"][:, cols] = act.astype(BF16)
         r["dpre"][:, cols] = d_pre
         r["sfc"][:, cols] = jnp.broadcast_to(
-            jnp.sum(d_pre.astype(F32), axis=0, keepdims=True), (8, 256)
+            jnp.sum(d_pre.astype(F32), axis=0, keepdims=True), (8, 512)
         )
 
         return c
 
-    lax.fori_loop(0, 8, ffn, 0)
+    lax.fori_loop(0, 4, ffn, 0)
 
     def ffn_dh(n, c):
         cols = pl.ds(pl.multiple_of(n * 256, 256), 256)
@@ -803,8 +838,8 @@
         out = []
         for i, (name, c0, n, rot) in enumerate(table):
             piece = Reduce(me, core, r[name], c0, n, rot, sems("rs"), (base + i) * 12)
-            k = (stage_at + i) * 9
-            out.append(piece.attach(stages[k : k + 9]))
+            k = (stage_at + i) * 5
+            out.append(piece.attach(stages[k : k + 5]))
         return out
 
     rp = reduces(REDUCE_P, 0, 0)
@@ -834,7 +869,7 @@
         r["dbr"][rows, :] = d_mid.astype(BF16)
         return c
 
-    rows_loop(T, 32, ln2_back)
+    rows_loop(T, 128, ln2_back)
 
     wor = r["wor"][...].reshape(HALF, D)
     r["datt"][...] = nt(wor, r["dbr"][...]).astype(BF16).reshape(8, HEAD, T)
@@ -845,6 +880,15 @@
     datt_swap.start()
     r["dz"][HEAD:, tok(j_me)] = r["datt"][j_me]
     r["dz"][0:HEAD, :] = jnp.zeros((HEAD, LEN), BF16)
+
+    gout = nn(r["attt"][...].reshape(HALF, T), r["dbr"][...]).astype(BF16)
+    left = gout[:, :HALF].reshape(2, 2, 4, 2, 16, HALF)
+    right = gout[:, HALF:].reshape(2, 2, 4, 2, 16, HALF)
+    go_at = r["g4"].at[pl.ds(2 * core, 2), :, :, :, :, pl.ds(GOUT0, HALF)]
+    go_at[...] = jnp.where(core == 0, left, right)
+    r["gos"][...] = jnp.where(core == 0, right, left)
+    px_go = pair(r["gos"], go_at, 7)
+    px_go.start()
 
     def grad_fc(t, c):
         cols = pl.ds(pl.multiple_of(GFC0 + t * 256, 256), 256)
@@ -858,6 +902,9 @@
     lax.fori_loop(0, 8, grad_fc, 0)
     for g in rf:
         g.start(0)
+    px_go.wait_recv()
+    for g in ro:
+        g.start(0)
 
     def ffn_out(n, c):
         cols = pl.ds(pl.multiple_of(n * 256, 256), 256)
@@ -868,18 +915,9 @@
     px_out = pair(r["outp"].at[their_rows], r["outr"], 6)
     px_out.start()
 
-    gout = nn(r["attt"][...].reshape(HALF, T), r["dbr"][...]).astype(BF16)
-    left = gout[:, :HALF].reshape(2, 2, 4, 2, 16, HALF)
-    right = gout[:, HALF:].reshape(2, 2, 4, 2, 16, HALF)
-    go_at = r["g4"].at[pl.ds(2 * core, 2), :, :, :, :, pl.ds(GOUT0, HALF)]
-    go_at[...] = jnp.where(core == 0, left, right)
-    r["gos"][...] = jnp.where(core == 0, right, left)
-    px_go = pair(r["gos"], go_at, 7)
-    px_go.start()
-
     def small2(i, c):
         s1, s2, s3, s4 = c
-        rows = pl.ds(pl.multiple_of(core * 128 + i * 32, 32), 32)
+        rows = pl.ds(pl.multiple_of(core * 128 + i * 128, 128), 128)
         dh = r["dhr"][rows, :]
         xhat, _ = norm_stats(r["middle"][rows, :])
         return (
@@ -890,30 +928,28 @@
         )
 
     zero = jnp.zeros((8, D), F32)
-    sums = lax.fori_loop(0, 4, small2, (zero, zero, zero, zero))
+    sums = lax.fori_loop(0, 1, small2, (zero, zero, zero, zero))
     for row, s in zip((1, 3, 6, 7), sums):
         r["sv"][row : row + 1, :] = jnp.sum(s, axis=0, keepdims=True)
 
     px_out.wait_recv()
 
     def block_out(i, c):
-        rows = pl.ds(pl.multiple_of(core * 128 + i * 32, 32), 32)
-        here = pl.ds(pl.multiple_of(i * 32, 32), 32)
+        rows = pl.ds(pl.multiple_of(core * 128 + i * 128, 128), 128)
+        here = pl.ds(pl.multiple_of(i * 128, 128), 128)
         o_block[here, :] = (
             r["middle"][rows, :] + (r["outp"][rows, :] + r["outr"][here, :]) + vrow(7)
         ).astype(BF16)
         return c
 
-    lax.fori_loop(0, 4, block_out, 0)
+    lax.fori_loop(0, 1, block_out, 0)
     px_out.wait_send()
 
     h_from(ym, every, 0, 128, 1)
     h_f[0].start()
     h_from(yp, every, 0, 128, 2)
     h_f[1].start()
-    px_go.wait_recv()
-    for g in ro:
-        g.start(0)
+    rf[0].forward(0)
     for g in rp:
         g.forward(0)
     datt_swap.wait()
@@ -950,19 +986,20 @@
         )
         r["dqt"][:, icols] = step(nfull, dq, True)
 
-        @pl.when(ib == 2)
-        def _():
-            rf[0].forward(0)
-
         @pl.when(ib == 6)
         def _():
             h_from(opposite, every, 0, 64, 3)
             h_from(opposite, every, 64, 64, 4)
             px_h.start()
 
-        @pl.when(ib == 5)
+        @pl.when(ib == 1)
         def _():
-            for g in rf[1:] + ro:
+            for g in rf[1:]:
+                g.forward(0)
+
+        @pl.when(ib == 4)
+        def _():
+            for g in ro:
                 g.forward(0)
 
         return c
@@ -992,14 +1029,9 @@
     gq_swap = dp_swap(1, lambda i: r["gqs"].at[i], lambda i: r["gqr"].at[i])
     gq_swap.start()
     r["gqr"][dp] = r["gqs"][dp]
-    for g in rp:
+    for g in rp + rf:
         g.finish(0)
         g.start(1)
-    for g in rf[:1]:
-        g.finish(0)
-        g.start(1)
-    for g in rp:
-        g.forward(1)
     dqkv_swap.wait()
 
     for k in range(3):
@@ -1012,12 +1044,10 @@
         r["dh1"][...] = v if k == 0 else r["dh1"][...] + v
     px_d1 = pair(r["dh1"].at[their_rows], r["dh1r"], 8)
     px_d1.start()
-    for g in rf[:1]:
-        g.forward(1)
-    for g in rf[1:] + ro:
+    for g in ro:
         g.finish(0)
         g.start(1)
-    for g in rp:
+    for g in rp + rf:
         g.finish(1)
         g.start(2)
     gq_swap.wait()
@@ -1029,26 +1059,19 @@
     gqt_swap = seq_swap(4, lambda j: r["gqt"].at[j], lambda j: r["finq"].at[j])
     gqt_swap.start()
     r["finq"][j_me] = r["gqt"][j_me]
-    for g in rf[:1]:
-        g.finish(1)
-        g.start(2)
-    for g in rf[1:] + ro:
-        g.forward(1)
-    for g in rp:
-        g.forward(2)
     px_d1.wait_recv()
 
     def ln1_back(i, c):
         s1, s2 = c
-        rows = pl.ds(pl.multiple_of(core * 128 + i * 32, 32), 32)
-        here = pl.ds(pl.multiple_of(i * 32, 32), 32)
+        rows = pl.ds(pl.multiple_of(core * 128 + i * 128, 128), 128)
+        here = pl.ds(pl.multiple_of(i * 128, 128), 128)
         dh = r["dh1"][rows, :] + r["dh1r"][here, :]
         xhat, inv = norm_stats(r["x"][rows, :].astype(F32))
         d_in = r["dmid"][rows, :] + norm_back(xhat, inv, dh, vrow(0))
         o_in[here, :] = d_in.astype(BF16)
         return s1 + fold8(dh * xhat), s2 + fold8(dh)
 
-    sums = lax.fori_loop(0, 4, ln1_back, (zero, zero))
+    sums = lax.fori_loop(0, 1, ln1_back, (zero, zero))
     for row, s in zip((0, 2), sums):
         r["sv"][row : row + 1, :] = jnp.sum(s, axis=0, keepdims=True)
 
@@ -1060,11 +1083,9 @@
     ss_swap = dp_swap(2, lambda i: r["ss"].at[i], lambda i: r["ssr"].at[i])
     ss_swap.start()
     r["ssr"][dp] = r["ss"][dp]
-    for g in rf[1:] + ro:
+    for g in ro:
         g.finish(1)
         g.start(2)
-    for g in rf[:1]:
-        g.forward(2)
     ss_swap.wait()
     r["st"][...] = jnp.sum(r["ssr"][...], axis=0)
     st_swap = seq_swap(5, lambda j: r["st"], lambda j: r["str"].at[j])
@@ -1073,8 +1094,6 @@
 
     mine8 = pl.ds(pl.multiple_of(core * 8, 8), 8)
     their8 = pl.ds(pl.multiple_of(8 - core * 8, 8), 8)
-    for g in rf[1:] + ro:
-        g.forward(2)
     gqt_swap.wait()
     px_q = pair(r["finq"].at[:, their8], o_wq.at[core], 11)
     px_q.start()

time: 172 us -> 168 us (0.977)
  Pallas kernels: 172 us -> 167 us
    pallas_call x1, Pallas kernels: 169 us -> 165 us  [block(): pl.pallas_call(kernel, out_shape=(jax.ShapeDtypeStruct((128, D), BF16), j...]
where the time goes in v3:
time: 168 us
  Pallas kernels  167 us (99%)
    pallas_call x1, Pallas kernels, block(): pl.pallas_call(kernel, out_shape=(jax.ShapeDtypeStruct((128, D), BF16), j...  165 us

profile of v3, /device:TPU:1, one launch (start us, length us, event | category | flops | bytes accessed | tf_op | source)
XLA Modules:
  0.0 167.8 jit_solution(16376728454773473001)
XLA Ops:
  0.6 164.9 %shard_map.194 = (bf16[128,1024]{1,0:T(8,128)(2,1)}, bf16[128,1024]{1,0:T(8,128)(2,1)}, f32[2,8,2560]{2,1,0:T(8,128)}, f32[2,8,8,256]{3,2,1,0:T(8,128)}, f32[32,1024]{1,0:T(8,128)}, /*index=5*/f32[8,128]{1,0:T(8,128)}) custom-call(bf16[8,3072]{1,0:T(8,128)(2,1)} %w_qkv.1, bf16[8,1024]{1,0:T(8,128)(2,1)} %w_out.1, bf16[8,4096]{1,0:T(8,128)(2,1)} %w_fc.1, ...), custom_call_target="tpu_custom_call" | custom-call | tf_op jit(solution)/shard_map/pallas_call | solution.py:1137
  165.5 2.3 %shard_map.195 = (bf16[128,1024]{1,0:T(8,128)(2,1)}, bf16[128,1024]{1,0:T(8,128)(2,1)}, f32[2,8]{1,0:T(2,128)}, f32[2,8]{1,0:T(2,128)}, f32[8,3072]{1,0:T(8,128)...) custom-call(bf16[128,1024]{1,0:T(8,128)(2,1)} %get-tuple-element.28., ...), custom_call_target="tpu_custom_call" | custom-call | tf_op jit(solution)/shard_map/pallas_call | solution.py:1159

commit v4 on v3

--- a/solution.py
+++ b/solution.py
@@ -596,6 +596,8 @@
         return out
 
     ga = gathers(GATHER_A, 0)
+    for g in ga:
+        g.direct = (0, 1)
     gb = gathers(GATHER_B, 3)
     gc = gathers(GATHER_C, 6)
     for g in ga + gb + gc:

time: 168 us -> 166 us (0.988)
  Pallas kernels: 167 us -> 165 us
    pallas_call x1, Pallas kernels: 165 us -> 163 us  [block(): pl.pallas_call(kernel, out_shape=(jax.ShapeDtypeStruct((128, D), BF16), j...]
where the time goes in v4:
time: 166 us
  Pallas kernels  165 us (99%)
    pallas_call x1, Pallas kernels, block(): pl.pallas_call(kernel, out_shape=(jax.ShapeDtypeStruct((128, D), BF16), j...  163 us

profile of v4, /device:TPU:1, one launch (start us, length us, event | category | flops | bytes accessed | tf_op | source)
XLA Modules:
  0.0 166.0 jit_solution(4224959915758769853)
XLA Ops:
  0.6 163.1 %shard_map.194 = (bf16[128,1024]{1,0:T(8,128)(2,1)}, bf16[128,1024]{1,0:T(8,128)(2,1)}, f32[2,8,2560]{2,1,0:T(8,128)}, f32[2,8,8,256]{3,2,1,0:T(8,128)}, f32[32,1024]{1,0:T(8,128)}, /*index=5*/f32[8,128]{1,0:T(8,128)}) custom-call(bf16[8,3072]{1,0:T(8,128)(2,1)} %w_qkv.1, bf16[8,1024]{1,0:T(8,128)(2,1)} %w_out.1, bf16[8,4096]{1,0:T(8,128)(2,1)} %w_fc.1, ...), custom_call_target="tpu_custom_call" | custom-call | tf_op jit(solution)/shard_map/pallas_call | solution.py:1139
  163.7 2.3 %shard_map.195 = (bf16[128,1024]{1,0:T(8,128)(2,1)}, bf16[128,1024]{1,0:T(8,128)(2,1)}, f32[2,8]{1,0:T(2,128)}, f32[2,8]{1,0:T(2,128)}, f32[8,3072]{1,0:T(8,128)...) custom-call(bf16[128,1024]{1,0:T(8,128)(2,1)} %get-tuple-element.28., ...), custom_call_target="tpu_custom_call" | custom-call | tf_op jit(solution)/shard_map/pallas_call | solution.py:1161
